TPU v7x, 32 devices: a whole 2x2x4 slice. The times are simulated.
32 devices in a mesh: lon: 8 (over y, x, core), lat: 4 (over z).
Axes of the slice: x: 2, y: 2, z: 4, core: 2. Of those that a mesh axis runs over, the one named last changes fastest.
Arguments:
- thermal_anomaly: float32 [46, 32, 1024], P(None, 'lat', 'lon'), may hold values from -6 to 6
- saltiness_anomaly: float32 [46, 32, 1024], P(None, 'lat', 'lon'), may hold values from -6 to 6
- zonal_volume_flux: float32 [46, 32, 1024], P(None, 'lat', 'lon'), may hold values from -0.2 to 0.2
- meridional_volume_flux: float32 [46, 32, 1024], P(None, 'lat', 'lon'), may hold values from -0.2 to 0.2
- vertical_diffusion_factor: float32 [46, 32, 1024], P(None, 'lat', 'lon'), may hold values from 0.05 to 5
- friction_factor: float32 [46, 32, 1024], P(None, 'lat', 'lon'), may hold values from 0.1 to 3
- seawater_indicator: int32 [32, 1024], P('lat', 'lon'), may hold values 0 or 1
- water_layer_depth: int32 [32, 1024], P('lat', 'lon'), may hold values from 1 to 46
Outputs:
- temperature_next: float32 [46, 32, 1024], P(None, 'lat', 'lon')
- salinity_next: float32 [46, 32, 1024], P(None, 'lat', 'lon')
All inputs are finite; a program needn't handle non-finite values. No bound on the sum of `seawater_indicator` on one device may be relied on, other than what follows from the above.
Results may differ from a plain program's by a relative error of at most 0.00002.
Values sent between devices are 32-bit elements; how exact they have to be, the bound alone decides.
A program may use at most 64 MiB of HBM per device.

v0:
```python
import jax
import jax.numpy as jnp
from jax import lax
from jax.sharding import PartitionSpec as P

SPLIT_PASSES = 4


DIFFUSE = 0.05


def partner(block, axis, stride):
    count = lax.axis_size(axis)
    route = []
    for low in range(count):
        high = low | 1 << stride
        if high != low and high < count:
            route += [(low, high), (high, low)]
    return lax.ppermute(block, axis, route)


def padded(cells, sides, width, closed):
    for axis, dim in sides:
        count = lax.axis_size(axis)
        ends = count if closed else count - 1
        head = lax.slice_in_dim(cells, 0, width, axis=dim)
        tail = lax.slice_in_dim(cells, cells.shape[dim] - width, cells.shape[dim], axis=dim)
        cells = jnp.concatenate(
            [
                lax.ppermute(tail, axis, [(i, (i + 1) % count) for i in range(ends)]),
                cells,
                lax.ppermute(head, axis, [((i + 1) % count, i) for i in range(ends)]),
            ],
            axis=dim,
        )
    return cells


def mirrored(stacked):
    top_rows = stacked[:, :, -1, :]
    bit_count = lax.axis_size("lon").bit_length() - 1
    swapped = top_rows
    for bit_index in range(bit_count):
        swapped = partner(swapped, "lon", bit_index)
    return swapped[:, :, ::-1]


def tridiagonal(lower_band, main_band, upper_band, right_side):
    water_layer_number = main_band.shape[0]
    sweep_ratio = upper_band[0] / main_band[0]
    sweep_value = right_side[:, 0] / main_band[0]
    ratio_list = [sweep_ratio]
    value_list = [sweep_value]
    for level_index in range(1, water_layer_number):
        pivot_value = main_band[level_index] - lower_band[level_index] * sweep_ratio
        sweep_ratio = upper_band[level_index] / pivot_value
        sweep_value = (
            right_side[:, level_index] - lower_band[level_index] * sweep_value
        ) / pivot_value
        ratio_list.append(sweep_ratio)
        value_list.append(sweep_value)
    solved_level = value_list[-1]
    solved_rows = [solved_level]
    for level_index in range(water_layer_number - 2, -1, -1):
        solved_level = value_list[level_index] - ratio_list[level_index] * solved_level
        solved_rows.append(solved_level)
    return jnp.stack(solved_rows[::-1], axis=1)


def face_terms(centre, west_side, east_side, south_side, north_side, hinge_parallels):
    east_flow = centre[0]
    north_flow = centre[1]
    seawater_sites = centre[2]
    open_east = seawater_sites * east_side[2]
    open_west = west_side[2] * seawater_sites
    open_north = seawater_sites * north_side[2]
    open_south = south_side[2] * seawater_sites
    flow_west_face = west_side[0]
    flow_south_face = south_side[1]
    flow_north_face = jnp.where(hinge_parallels, 0.5 * (north_flow - north_side[1]), north_flow)
    return (
        open_east,
        open_west,
        open_north,
        open_south,
        east_flow,
        flow_west_face,
        flow_north_face,
        flow_south_face,
    )


def advance(scalar_quantities, west_tr, east_tr, south_tr, north_tr, faces):
    (
        open_east,
        open_west,
        open_north,
        open_south,
        east_flow,
        flow_west_face,
        flow_north_face,
        flow_south_face,
    ) = faces
    flux_east = open_east * (
        jnp.maximum(east_flow, 0.0) * scalar_quantities
        + jnp.minimum(east_flow, 0.0) * east_tr
        - DIFFUSE * (east_tr - scalar_quantities)
    )
    flux_west = open_west * (
        jnp.maximum(flow_west_face, 0.0) * west_tr
        + jnp.minimum(flow_west_face, 0.0) * scalar_quantities
        - DIFFUSE * (scalar_quantities - west_tr)
    )
    flux_north = open_north * (
        jnp.maximum(flow_north_face, 0.0) * scalar_quantities
        + jnp.minimum(flow_north_face, 0.0) * north_tr
        - DIFFUSE * (north_tr - scalar_quantities)
    )
    flux_south = open_south * (
        jnp.maximum(flow_south_face, 0.0) * south_tr
        + jnp.minimum(flow_south_face, 0.0) * scalar_quantities
        - DIFFUSE * (scalar_quantities - south_tr)
    )
    return scalar_quantities - (flux_east - flux_west + flux_north - flux_south)


def shards(
    thermal_anomaly,
    saltiness_anomaly,
    zonal_volume_flux,
    meridional_volume_flux,
    vertical_diffusion_factor,
    friction_factor,
    seawater_indicator,
    water_layer_depth,
):
    is_top = lax.axis_index("lat") == lax.axis_size("lat") - 1
    partition_parallels = thermal_anomaly.shape[1]
    hinge_parallels = (
        is_top & (jnp.arange(partition_parallels) == partition_parallels - 1)[None, :, None]
    )

    def vertical_pair(stacked):
        lat_ext = padded(stacked, (("lat", 2),), 1, False)
        fold_data = mirrored(stacked)
        north_rim = jnp.where(is_top, fold_data, lat_ext[:, :, -1, :])
        north_side = jnp.concatenate([lat_ext[:, :, 2:-1, :], north_rim[:, :, None, :]], axis=2)
        return (lat_ext[:, :, :-2, :], north_side)

    water_layer_number = thermal_anomaly.shape[0]
    depth_index = jnp.arange(water_layer_number, dtype=jnp.int32)[:, None, None]
    seawater_sites = jnp.where(
        (seawater_indicator[None] == 1) & (depth_index < water_layer_depth[None]), 1.0, 0.0
    ).astype(jnp.float32)
    damping = 1.0 + friction_factor
    east_flow = zonal_volume_flux / damping
    north_flow = meridional_volume_flux / damping

    def neighbour_sites(stacked):
        cycle_ext = padded(stacked, (("lon", 3),), 1, True)
        south_side, north_side = vertical_pair(stacked)
        return (cycle_ext[..., :-2], cycle_ext[..., 2:], south_side, north_side)

    fields = jnp.stack([east_flow, north_flow, seawater_sites])
    west_side, east_side, south_side, north_side = neighbour_sites(fields)
    faces = face_terms(fields, west_side, east_side, south_side, north_side, hinge_parallels)
    scalar_quantities = jnp.stack([thermal_anomaly, saltiness_anomaly]) * seawater_sites
    for substep in range(SPLIT_PASSES):
        west_tr, east_tr, south_tr, north_tr = neighbour_sites(scalar_quantities)
        scalar_quantities = advance(scalar_quantities, west_tr, east_tr, south_tr, north_tr, faces)
    (
        open_east,
        open_west,
        open_north,
        open_south,
        east_face,
        flow_west_face,
        flow_north_face,
        flow_south_face,
    ) = faces
    divergence = (
        open_east * east_face
        - open_west * flow_west_face
        + open_north * flow_north_face
        - open_south * flow_south_face
    )
    deeper_sum = jnp.cumsum(divergence[::-1], axis=0)[::-1]
    zero_face = jnp.zeros_like(deeper_sum[:1])
    transport = -float(SPLIT_PASSES) * jnp.concatenate(
        [zero_face, deeper_sum[1:], zero_face], axis=0
    )
    mixing_faces = jnp.concatenate(
        [
            zero_face,
            vertical_diffusion_factor[:-1] * seawater_sites[:-1] * seawater_sites[1:],
            zero_face,
        ],
        axis=0,
    )
    main_band = (
        1.0
        - jnp.minimum(transport[1:], 0.0)
        + mixing_faces[1:]
        + jnp.maximum(transport[:-1], 0.0)
        + mixing_faces[:-1]
    )
    upper_band = -(jnp.maximum(transport[1:], 0.0) + mixing_faces[1:])
    lower_band = jnp.minimum(transport[:-1], 0.0) - mixing_faces[:-1]
    solved = tridiagonal(lower_band, main_band, upper_band, scalar_quantities)
    return (solved[0], solved[1])


def solution(mesh):
    in_specs = (
        P(None, "lat", "lon"),
        P(None, "lat", "lon"),
        P(None, "lat", "lon"),
        P(None, "lat", "lon"),
        P(None, "lat", "lon"),
        P(None, "lat", "lon"),
        P("lat", "lon"),
        P("lat", "lon"),
    )
    out_specs = (P(None, "lat", "lon"), P(None, "lat", "lon"))
    return jax.shard_map(shards, mesh=mesh, in_specs=in_specs, out_specs=out_specs, check_vma=False)
```

profile of v0, /device:TPU:0, one launch (start us, length us, event | category | flops | bytes accessed | tf_op | source)
XLA Modules:
  0.0 170.3 jit_solution(10814465534048532484)
XLA Ops:
  2.8 4.9 %collective-permute-start.12 = (f32[3,46,1,128]{3,1,0,2:T(8,128)S(1)}, f32[3,46,1,128]{3,1,0,2:T(8,128)S(1)}, u32[]{:S(2)}, u32[]{:S(2)}) collective-permute-start(f32[3,46,1,128]{3,1,0,2:T(8,128)S(1)} %copy.1015), channel_id=1, source_target_pairs={{0,1},{1,2},{2,3},{4,5},{5,6},{6,7},{8,9},{9,10},{10,11},{12,13},{... | collective-permute-start | bytes 211976 | tf_op jit(solution)/shard_map/ppermute | solution.py:30
  10.5 2.2 %collective-permute-start = (f32[3,46,8,1]{1,2,3,0:T(8,128)S(1)}, f32[3,46,8,1]{1,2,3,0:T(8,128)S(1)}, u32[]{:S(2)}, u32[]{:S(2)}) collective-permute-start(f32[3,46,8,1]{1,2,3,0:T(8,128)S(1)} %copy.889), channel_id=1, source_target_pairs={{4,0},{8,4},{12,8},{16,12},{20,16},{24,20},{28,24},{0,28},{5,1},{9... | collective-permute-start | bytes 13256 | tf_op jit(solution)/shard_map/ppermute | solution.py:32
  15.6 1.4 collective-permute-done.5
  17.0 1.5 collective-permute-start.6
  19.3 2.1 %collective-permute-done.6 = f32[3,46,128]{2,1,0:T(8,128)S(1)} collective-permute-done((f32[3,46,128]{2,1,0:T(8,128)S(1)}, f32[3,46,128]{2,1,0:T(8,128)S(1)}, u32[]{:S(2)}, u32[]{:S(2)}) %collective-permute-start.6) | collective-permute-done | bytes 70688 | tf_op jit(solution)/shard_map/ppermute | solution.py:19
  27.0 5.2 %collective-permute-start.13 = (f32[2,46,1,128]{3,2,1,0:T(1,128)S(1)}, f32[2,46,1,128]{3,2,1,0:T(1,128)}, u32[]{:S(2)}, u32[]{:S(2)}) collective-permute-start(f32[2,46,1,128]{3,2,1,0:T(1,128)S(1)} %get-tuple-element.161), channel_id=1, source_target_pairs={{0,1},{1,2},{2,3},{4,5},{5,6},{6,7},{8,9},{9,10},{10,11},{12,13},{... | collective-permute-start | bytes 141320 | tf_op jit(solution)/shard_map/ppermute | solution.py:30
  33.1 3.5 %fusion.379 = f32[46,8,128]{2,1,0:T(8,128)S(1)} fusion(f32[46,8,128]{2,1,0:T(8,128)S(1)} %rev.24), kind=kOutput, calls=%fused_computation.735 | output fusion | flops 2119680 | bytes 376832 | tf_op jit(solution)/shard_map/jit(cumsum)/reduce_window_sum | solution.py:187
  52.4 2.3 %collective-permute-done.9 = f32[2,46,128]{2,1,0:T(8,128)S(1)} collective-permute-done((f32[2,46,128]{2,1,0:T(8,128)S(1)}, f32[2,46,128]{2,1,0:T(8,128)S(1)}, u32[]{:S(2)}, u32[]{:S(2)}) %collective-permute-start.9) | collective-permute-done | bytes 47136 | tf_op jit(solution)/shard_map/ppermute | solution.py:19
  54.7 1.5 collective-permute-start.10
  60.6 6.5 %collective-permute-done.1 = f32[2,46,8,1]{3,2,1,0:T(8,128)} collective-permute-done((f32[2,46,8,1]{3,2,1,0:T(8,128)}, f32[2,46,8,1]{3,2,1,0:T(8,128)}, u32[]{:S(2)}, u32[]{:S(2)}) %collective-permute-start.1) | collective-permute-done | bytes 2976 | tf_op jit(solution)/shard_map/ppermute | solution.py:32
  67.1 1.5 collective-permute-done.3
  68.7 1.9 %fusion.30 = f32[2,46,8,128]{3,2,1,0:T(8,128)S(1)} fusion(f32[2,46,8,128]{3,2,1,0:T(8,128)S(1)} %maximum_multiply_fusion, f32[2,46,1,128]{3,2,1,0:T(1,128)} %collective-permute-done.13, f32[2,46,1,128]{3,2,1,0:T(1,128)S(1)} %copy.895, f32[2,46,7,128]{3,2,1,0:T(8,128)} %slice.1022, f32[2,46,8,1]{3,2,1,0:T(8,128)} %collective-permute-done.3, ...), kind=kLoop, calls=%fused_computation.41 | loop fusion | flops 3391488 | bytes 3444480 | tf_op jit(solution)/shard_map/sub | solution.py:124
  71.3 1.3 fusion.337
  73.6 1.4 fusion.339
  75.0 5.2 %collective-permute-start.20 = (f32[2,46,1,128]{3,2,1,0:T(1,128)S(1)}, f32[2,46,1,128]{3,2,1,0:T(1,128)}, u32[]{:S(2)}, u32[]{:S(2)}) collective-permute-start(f32[2,46,1,128]{3,2,1,0:T(1,128)S(1)} %get-tuple-element.157), channel_id=1, source_target_pairs={{0,1},{1,2},{2,3},{4,5},{5,6},{6,7},{8,9},{9,10},{10,11},{12,13},{... | collective-permute-start | bytes 141320 | tf_op jit(solution)/shard_map/ppermute | solution.py:30
  87.5 6.9 %collective-permute-done.14 = f32[2,46,8,1]{3,2,1,0:T(8,128)} collective-permute-done((f32[2,46,8,1]{3,2,1,0:T(8,128)}, f32[2,46,8,1]{3,2,1,0:T(8,128)}, u32[]{:S(2)}, u32[]{:S(2)}) %collective-permute-start.14) | collective-permute-done | bytes 2976 | tf_op jit(solution)/shard_map/ppermute | solution.py:32
  94.4 1.5 collective-permute-done.15
  96.6 1.9 %fusion.22 = f32[2,46,8,128]{3,2,1,0:T(8,128)S(1)} fusion(f32[2,46,8,128]{3,2,1,0:T(8,128)S(1)} %fusion.30, f32[2,46,1,128]{3,2,1,0:T(1,128)} %collective-permute-done.20, f32[2,46,1,128]{3,2,1,0:T(1,128)S(1)} %copy.897, f32[2,46,7,128]{3,2,1,0:T(8,128)} %slice.1027, f32[2,46,8,1]{3,2,1,0:T(8,128)} %copy-done.8, f32[2,46,8,1]{3,2,1,0:T(8,128)} %collective-permute-done.14, ...), kind=kLoop, calls=%fused_computation.30 | loop fusion | flops 3391488 | bytes 3444480 | tf_op jit(solution)/shard_map/sub | solution.py:124
  99.2 1.4 fusion.340
  100.5 1.4 collective-permute-start.24
  102.7 1.3 subtract_bitcast_fusion
  104.0 4.9 %collective-permute-start.27 = (f32[2,46,1,128]{3,2,1,0:T(1,128)S(1)}, f32[2,46,1,128]{3,2,1,0:T(1,128)}, u32[]{:S(2)}, u32[]{:S(2)}) collective-permute-start(f32[2,46,1,128]{3,2,1,0:T(1,128)S(1)} %get-tuple-element.153), channel_id=1, source_target_pairs={{0,1},{1,2},{2,3},{4,5},{5,6},{6,7},{8,9},{9,10},{10,11},{12,13},{... | collective-permute-start | bytes 141320 | tf_op jit(solution)/shard_map/ppermute | solution.py:30
  116.2 6.6 %collective-permute-done.21 = f32[2,46,8,1]{3,2,1,0:T(8,128)S(1)} collective-permute-done((f32[2,46,8,1]{3,2,1,0:T(8,128)}, f32[2,46,8,1]{3,2,1,0:T(8,128)S(1)}, u32[]{:S(2)}, u32[]{:S(2)}) %collective-permute-start.21) | collective-permute-done | bytes 2976 | tf_op jit(solution)/shard_map/ppermute | solution.py:32
  122.8 1.5 collective-permute-done.22
  124.3 1.9 %fusion.14 = f32[2,46,8,128]{3,2,1,0:T(8,128)S(1)} fusion(f32[2,46,8,128]{3,2,1,0:T(8,128)S(1)} %fusion.22, f32[2,46,1,128]{3,2,1,0:T(1,128)} %collective-permute-done.27, f32[2,46,1,128]{3,2,1,0:T(1,128)S(1)} %copy.898, f32[2,46,7,128]{3,2,1,0:T(8,128)} %slice.1032, f32[2,46,8,1]{3,2,1,0:T(8,128)} %collective-permute-done.22, f32[2,46,8,1]{3,2,1,0:T(8,128)} %copy-done.7, ...), kind=kLoop, calls=%fused_computation.19 | loop fusion | flops 3391488 | bytes 3444480 | tf_op jit(solution)/shard_map/sub | solution.py:124
  128.1 1.7 collective-permute-start.31
  129.8 4.9 %collective-permute-start.34 = (f32[2,46,1,128]{3,2,1,0:T(1,128)S(1)}, f32[2,46,1,128]{3,2,1,0:T(1,128)}, u32[]{:S(2)}, u32[]{:S(2)}) collective-permute-start(f32[2,46,1,128]{3,2,1,0:T(1,128)S(1)} %get-tuple-element.149), channel_id=1, source_target_pairs={{0,1},{1,2},{2,3},{4,5},{5,6},{6,7},{8,9},{9,10},{10,11},{12,13},{... | collective-permute-start | bytes 141320 | tf_op jit(solution)/shard_map/ppermute | solution.py:30
  138.3 1.9 %collective-permute-done.32 = f32[2,46,128]{2,1,0:T(8,128)} collective-permute-done((f32[2,46,128]{2,1,0:T(8,128)S(1)}, f32[2,46,128]{2,1,0:T(8,128)}, u32[]{:S(2)}, u32[]{:S(2)}) %collective-permute-start.32) | collective-permute-done | bytes 47136 | tf_op jit(solution)/shard_map/ppermute | solution.py:19
  142.0 5.0 %collective-permute-done.28 = f32[2,46,8,1]{3,2,1,0:T(8,128)S(1)} collective-permute-done((f32[2,46,8,1]{3,2,1,0:T(8,128)}, f32[2,46,8,1]{3,2,1,0:T(8,128)S(1)}, u32[]{:S(2)}, u32[]{:S(2)}) %collective-permute-start.28) | collective-permute-done | bytes 2976 | tf_op jit(solution)/shard_map/ppermute | solution.py:32
  147.0 2.6 %collective-permute-done.29 = f32[2,46,8,1]{3,2,1,0:T(8,128)} collective-permute-done((f32[2,46,8,1]{3,2,1,0:T(8,128)}, f32[2,46,8,1]{3,2,1,0:T(8,128)}, u32[]{:S(2)}, u32[]{:S(2)}) %collective-permute-start.29) | collective-permute-done | bytes 2976 | tf_op jit(solution)/shard_map/ppermute | solution.py:30
  149.6 1.6 fusion.6
  152.3 1.6 constant_dynamic-update-slice_fusion.45
  (456 shorter events, 77.2 us)
Async XLA Ops:
  2.8 12.8 %collective-permute-start.12 = (f32[3,46,1,128]{3,1,0,2:T(8,128)S(1)}, f32[3,46,1,128]{3,1,0,2:T(8,128)S(1)}, u32[]{:S(2)}, u32[]{:S(2)}) collective-permute-start(f32[3,46,1,128]{3,1,0,2:T(8,128)S(1)} %copy.1015), channel_id=1, source_target_pairs={{0,1},{1,2},{2,3},{4,5},{5,6},{6,7},{8,9},{9,10},{10,11},{12,13},{... | collective-permute-start | bytes 211976 | tf_op jit(solution)/shard_map/ppermute | solution.py:30
  7.7 5.0 %collective-permute-start.4 = (f32[3,46,128]{2,1,0:T(8,128)S(1)}, f32[3,46,128]{2,1,0:T(8,128)S(1)}, u32[]{:S(2)}, u32[]{:S(2)}) collective-permute-start(f32[3,46,128]{2,1,0:T(8,128)S(1)} %bitcast.1860), channel_id=1, source_target_pairs={{0,4},{4,0},{8,12},{12,8},{16,20},{20,16},{24,28},{28,24},{1,5},{5... | collective-permute-start | bytes 211976 | tf_op jit(solution)/shard_map/ppermute | solution.py:19
  7.8 13.7 %collective-permute-start.7 = (f32[3,46,1,128]{3,1,0,2:T(8,128)S(1)}, f32[3,46,1,128]{3,1,0,2:T(8,128)S(1)}, u32[]{:S(2)}, u32[]{:S(2)}) collective-permute-start(f32[3,46,1,128]{3,1,0,2:T(8,128)S(1)} %copy.955), channel_id=1, source_target_pairs={{1,0},{2,1},{3,2},{5,4},{6,5},{7,6},{9,8},{10,9},{11,10},{13,12},{... | collective-permute-start | bytes 211976 | tf_op jit(solution)/shard_map/ppermute | solution.py:32
  9.6 4.7 %collective-permute-start.2 = (f32[3,46,8,1]{1,2,3,0:T(8,128)S(1)}, f32[3,46,8,1]{1,2,3,0:T(8,128)S(1)}, u32[]{:S(2)}, u32[]{:S(2)}) collective-permute-start(f32[3,46,8,1]{1,2,3,0:T(8,128)S(1)} %copy.891), channel_id=1, source_target_pairs={{0,4},{4,8},{8,12},{12,16},{16,20},{20,24},{24,28},{28,0},{1,5},{5... | collective-permute-start | bytes 13256 | tf_op jit(solution)/shard_map/ppermute | solution.py:30
  10.5 3.6 %collective-permute-start = (f32[3,46,8,1]{1,2,3,0:T(8,128)S(1)}, f32[3,46,8,1]{1,2,3,0:T(8,128)S(1)}, u32[]{:S(2)}, u32[]{:S(2)}) collective-permute-start(f32[3,46,8,1]{1,2,3,0:T(8,128)S(1)} %copy.889), channel_id=1, source_target_pairs={{4,0},{8,4},{12,8},{16,12},{20,16},{24,20},{28,24},{0,28},{5,1},{9... | collective-permute-start | bytes 13256 | tf_op jit(solution)/shard_map/ppermute | solution.py:32
  12.7 4.4 %collective-permute-start.5 = (f32[3,46,128]{2,1,0:T(8,128)S(1)}, f32[3,46,128]{2,1,0:T(8,128)S(1)}, u32[]{:S(2)}, u32[]{:S(2)}) collective-permute-start(f32[3,46,128]{2,1,0:T(8,128)S(1)} %collective-permute-done.4), channel_id=1, source_target_pairs={{0,8},{8,0},{4,12},{12,4},{16,24},{24,16},{20,28},{28,20},{1,9},{9... | collective-permute-start | bytes 211976 | tf_op jit(solution)/shard_map/ppermute | solution.py:19
  17.0 4.4 %collective-permute-start.6 = (f32[3,46,128]{2,1,0:T(8,128)S(1)}, f32[3,46,128]{2,1,0:T(8,128)S(1)}, u32[]{:S(2)}, u32[]{:S(2)}) collective-permute-start(f32[3,46,128]{2,1,0:T(8,128)S(1)} %collective-permute-done.5), channel_id=1, source_target_pairs={{0,16},{16,0},{4,20},{20,4},{8,24},{24,8},{12,28},{28,12},{1,17},{... | collective-permute-start | bytes 211976 | tf_op jit(solution)/shard_map/ppermute | solution.py:19
  27.0 41.7 %collective-permute-start.13 = (f32[2,46,1,128]{3,2,1,0:T(1,128)S(1)}, f32[2,46,1,128]{3,2,1,0:T(1,128)}, u32[]{:S(2)}, u32[]{:S(2)}) collective-permute-start(f32[2,46,1,128]{3,2,1,0:T(1,128)S(1)} %get-tuple-element.161), channel_id=1, source_target_pairs={{0,1},{1,2},{2,3},{4,5},{5,6},{6,7},{8,9},{9,10},{10,11},{12,13},{... | collective-permute-start | bytes 141320 | tf_op jit(solution)/shard_map/ppermute | solution.py:30
  37.6 22.1 %collective-permute-start.11 = (f32[2,46,1,128]{3,2,1,0:T(1,128)}, f32[2,46,1,128]{3,2,1,0:T(1,128)}, u32[]{:S(2)}, u32[]{:S(2)}) collective-permute-start(f32[2,46,1,128]{3,2,1,0:T(1,128)} %get-tuple-element.160), channel_id=1, source_target_pairs={{1,0},{2,1},{3,2},{5,4},{6,5},{7,6},{9,8},{10,9},{11,10},{13,12},{... | collective-permute-start | bytes 141320 | tf_op jit(solution)/shard_map/ppermute | solution.py:32
  38.9 11.5 %collective-permute-start.8 = (f32[2,46,128]{2,1,0:T(8,128)}, f32[2,46,128]{2,1,0:T(8,128)S(1)}, u32[]{:S(2)}, u32[]{:S(2)}) collective-permute-start(f32[2,46,128]{2,1,0:T(8,128)} %bitcast.1853), channel_id=1, source_target_pairs={{0,4},{4,0},{8,12},{12,8},{16,20},{20,16},{24,28},{28,24},{1,5},{5... | collective-permute-start | bytes 141320 | tf_op jit(solution)/shard_map/ppermute | solution.py:19
  50.5 4.2 %collective-permute-start.9 = (f32[2,46,128]{2,1,0:T(8,128)S(1)}, f32[2,46,128]{2,1,0:T(8,128)S(1)}, u32[]{:S(2)}, u32[]{:S(2)}) collective-permute-start(f32[2,46,128]{2,1,0:T(8,128)S(1)} %collective-permute-done.8), channel_id=1, source_target_pairs={{0,8},{8,0},{4,12},{12,4},{16,24},{24,16},{20,28},{28,20},{1,9},{9... | collective-permute-start | bytes 141320 | tf_op jit(solution)/shard_map/ppermute | solution.py:19
  54.7 4.2 %collective-permute-start.10 = (f32[2,46,128]{2,1,0:T(8,128)S(1)}, f32[2,46,128]{2,1,0:T(8,128)}, u32[]{:S(2)}, u32[]{:S(2)}) collective-permute-start(f32[2,46,128]{2,1,0:T(8,128)S(1)} %collective-permute-done.9), channel_id=1, source_target_pairs={{0,16},{16,0},{4,20},{20,4},{8,24},{24,8},{12,28},{28,12},{1,17},{... | collective-permute-start | bytes 141320 | tf_op jit(solution)/shard_map/ppermute | solution.py:19
  57.6 9.5 %collective-permute-start.1 = (f32[2,46,8,1]{3,2,1,0:T(8,128)}, f32[2,46,8,1]{3,2,1,0:T(8,128)}, u32[]{:S(2)}, u32[]{:S(2)}) collective-permute-start(f32[2,46,8,1]{3,2,1,0:T(8,128)} %get-tuple-element.158), channel_id=1, source_target_pairs={{4,0},{8,4},{12,8},{16,12},{20,16},{24,20},{28,24},{0,28},{5,1},{9... | collective-permute-start | bytes 8840 | tf_op jit(solution)/shard_map/ppermute | solution.py:32
  57.9 10.7 %collective-permute-start.3 = (f32[2,46,8,1]{3,2,1,0:T(8,128)S(1)}, f32[2,46,8,1]{3,2,1,0:T(8,128)}, u32[]{:S(2)}, u32[]{:S(2)}) collective-permute-start(f32[2,46,8,1]{3,2,1,0:T(8,128)S(1)} %copy-done.6), channel_id=1, source_target_pairs={{0,4},{4,8},{8,12},{12,16},{16,20},{20,24},{24,28},{28,0},{1,5},{5... | collective-permute-start | bytes 8840 | tf_op jit(solution)/shard_map/ppermute | solution.py:30
  72.6 8.9 %collective-permute-start.17 = (f32[2,46,128]{2,1,0:T(8,128)S(1)}, f32[2,46,128]{2,1,0:T(8,128)S(1)}, u32[]{:S(2)}, u32[]{:S(2)}) collective-permute-start(f32[2,46,128]{2,1,0:T(8,128)S(1)} %collective-permute-done.16), channel_id=1, source_target_pairs={{0,8},{8,0},{4,12},{12,4},{16,24},{24,16},{20,28},{28,20},{1,9},{9... | collective-permute-start | bytes 141320 | tf_op jit(solution)/shard_map/ppermute | solution.py:19
  75.0 21.6 %collective-permute-start.20 = (f32[2,46,1,128]{3,2,1,0:T(1,128)S(1)}, f32[2,46,1,128]{3,2,1,0:T(1,128)}, u32[]{:S(2)}, u32[]{:S(2)}) collective-permute-start(f32[2,46,1,128]{3,2,1,0:T(1,128)S(1)} %get-tuple-element.157), channel_id=1, source_target_pairs={{0,1},{1,2},{2,3},{4,5},{5,6},{6,7},{8,9},{9,10},{10,11},{12,13},{... | collective-permute-start | bytes 141320 | tf_op jit(solution)/shard_map/ppermute | solution.py:30
  80.2 6.4 %collective-permute-start.19 = (f32[2,46,1,128]{3,2,1,0:T(1,128)}, f32[2,46,1,128]{3,2,1,0:T(1,128)}, u32[]{:S(2)}, u32[]{:S(2)}) collective-permute-start(f32[2,46,1,128]{3,2,1,0:T(1,128)} %get-tuple-element.156), channel_id=1, source_target_pairs={{1,0},{2,1},{3,2},{5,4},{6,5},{7,6},{9,8},{10,9},{11,10},{13,12},{... | collective-permute-start | bytes 141320 | tf_op jit(solution)/shard_map/ppermute | solution.py:32
  81.5 4.3 %collective-permute-start.18 = (f32[2,46,128]{2,1,0:T(8,128)S(1)}, f32[2,46,128]{2,1,0:T(8,128)}, u32[]{:S(2)}, u32[]{:S(2)}) collective-permute-start(f32[2,46,128]{2,1,0:T(8,128)S(1)} %collective-permute-done.17), channel_id=1, source_target_pairs={{0,16},{16,0},{4,20},{20,4},{8,24},{24,8},{12,28},{28,12},{1,17},{... | collective-permute-start | bytes 141320 | tf_op jit(solution)/shard_map/ppermute | solution.py:19
  84.5 9.9 %collective-permute-start.14 = (f32[2,46,8,1]{3,2,1,0:T(8,128)}, f32[2,46,8,1]{3,2,1,0:T(8,128)}, u32[]{:S(2)}, u32[]{:S(2)}) collective-permute-start(f32[2,46,8,1]{3,2,1,0:T(8,128)} %get-tuple-element.154), channel_id=1, source_target_pairs={{4,0},{8,4},{12,8},{16,12},{20,16},{24,20},{28,24},{0,28},{5,1},{9... | collective-permute-start | bytes 8840 | tf_op jit(solution)/shard_map/ppermute | solution.py:32
  85.0 10.9 %collective-permute-start.15 = (f32[2,46,8,1]{3,2,1,0:T(8,128)}, f32[2,46,8,1]{3,2,1,0:T(8,128)S(1)}, u32[]{:S(2)}, u32[]{:S(2)}) collective-permute-start(f32[2,46,8,1]{3,2,1,0:T(8,128)} %get-tuple-element.155), channel_id=1, source_target_pairs={{0,4},{4,8},{8,12},{12,16},{16,20},{20,24},{24,28},{28,0},{1,5},{5... | collective-permute-start | bytes 8840 | tf_op jit(solution)/shard_map/ppermute | solution.py:30
  100.5 9.6 %collective-permute-start.24 = (f32[2,46,128]{2,1,0:T(8,128)S(1)}, f32[2,46,128]{2,1,0:T(8,128)S(1)}, u32[]{:S(2)}, u32[]{:S(2)}) collective-permute-start(f32[2,46,128]{2,1,0:T(8,128)S(1)} %collective-permute-done.23), channel_id=1, source_target_pairs={{0,8},{8,0},{4,12},{12,4},{16,24},{24,16},{20,28},{28,20},{1,9},{9... | collective-permute-start | bytes 141320 | tf_op jit(solution)/shard_map/ppermute | solution.py:19
  104.0 20.3 %collective-permute-start.27 = (f32[2,46,1,128]{3,2,1,0:T(1,128)S(1)}, f32[2,46,1,128]{3,2,1,0:T(1,128)}, u32[]{:S(2)}, u32[]{:S(2)}) collective-permute-start(f32[2,46,1,128]{3,2,1,0:T(1,128)S(1)} %get-tuple-element.153), channel_id=1, source_target_pairs={{0,1},{1,2},{2,3},{4,5},{5,6},{6,7},{8,9},{9,10},{10,11},{12,13},{... | collective-permute-start | bytes 141320 | tf_op jit(solution)/shard_map/ppermute | solution.py:30
  108.9 6.4 %collective-permute-start.26 = (f32[2,46,1,128]{3,2,1,0:T(1,128)}, f32[2,46,1,128]{3,2,1,0:T(1,128)}, u32[]{:S(2)}, u32[]{:S(2)}) collective-permute-start(f32[2,46,1,128]{3,2,1,0:T(1,128)} %get-tuple-element.152), channel_id=1, source_target_pairs={{1,0},{2,1},{3,2},{5,4},{6,5},{7,6},{9,8},{10,9},{11,10},{13,12},{... | collective-permute-start | bytes 141320 | tf_op jit(solution)/shard_map/ppermute | solution.py:32
  110.2 4.3 %collective-permute-start.25 = (f32[2,46,128]{2,1,0:T(8,128)S(1)}, f32[2,46,128]{2,1,0:T(8,128)}, u32[]{:S(2)}, u32[]{:S(2)}) collective-permute-start(f32[2,46,128]{2,1,0:T(8,128)S(1)} %collective-permute-done.24), channel_id=1, source_target_pairs={{0,16},{16,0},{4,20},{20,4},{8,24},{24,8},{12,28},{28,12},{1,17},{... | collective-permute-start | bytes 141320 | tf_op jit(solution)/shard_map/ppermute | solution.py:19
  112.7 10.1 %collective-permute-start.21 = (f32[2,46,8,1]{3,2,1,0:T(8,128)}, f32[2,46,8,1]{3,2,1,0:T(8,128)S(1)}, u32[]{:S(2)}, u32[]{:S(2)}) collective-permute-start(f32[2,46,8,1]{3,2,1,0:T(8,128)} %get-tuple-element.150), channel_id=1, source_target_pairs={{4,0},{8,4},{12,8},{16,12},{20,16},{24,20},{28,24},{0,28},{5,1},{9... | collective-permute-start | bytes 8840 | tf_op jit(solution)/shard_map/ppermute | solution.py:32
  113.4 10.9 %collective-permute-start.22 = (f32[2,46,8,1]{3,2,1,0:T(8,128)}, f32[2,46,8,1]{3,2,1,0:T(8,128)}, u32[]{:S(2)}, u32[]{:S(2)}) collective-permute-start(f32[2,46,8,1]{3,2,1,0:T(8,128)} %get-tuple-element.151), channel_id=1, source_target_pairs={{0,4},{4,8},{8,12},{12,16},{16,20},{20,24},{24,28},{28,0},{1,5},{5... | collective-permute-start | bytes 8840 | tf_op jit(solution)/shard_map/ppermute | solution.py:30
  128.1 7.9 %collective-permute-start.31 = (f32[2,46,128]{2,1,0:T(8,128)S(1)}, f32[2,46,128]{2,1,0:T(8,128)S(1)}, u32[]{:S(2)}, u32[]{:S(2)}) collective-permute-start(f32[2,46,128]{2,1,0:T(8,128)S(1)} %collective-permute-done.30), channel_id=1, source_target_pairs={{0,8},{8,0},{4,12},{12,4},{16,24},{24,16},{20,28},{28,20},{1,9},{9... | collective-permute-start | bytes 141320 | tf_op jit(solution)/shard_map/ppermute | solution.py:19
  129.8 19.8 %collective-permute-start.34 = (f32[2,46,1,128]{3,2,1,0:T(1,128)S(1)}, f32[2,46,1,128]{3,2,1,0:T(1,128)}, u32[]{:S(2)}, u32[]{:S(2)}) collective-permute-start(f32[2,46,1,128]{3,2,1,0:T(1,128)S(1)} %get-tuple-element.149), channel_id=1, source_target_pairs={{0,1},{1,2},{2,3},{4,5},{5,6},{6,7},{8,9},{9,10},{10,11},{12,13},{... | collective-permute-start | bytes 141320 | tf_op jit(solution)/shard_map/ppermute | solution.py:30
  134.7 6.4 %collective-permute-start.33 = (f32[2,46,1,128]{3,2,1,0:T(1,128)}, f32[2,46,1,128]{3,2,1,0:T(1,128)}, u32[]{:S(2)}, u32[]{:S(2)}) collective-permute-start(f32[2,46,1,128]{3,2,1,0:T(1,128)} %get-tuple-element.148), channel_id=1, source_target_pairs={{1,0},{2,1},{3,2},{5,4},{6,5},{7,6},{9,8},{10,9},{11,10},{13,12},{... | collective-permute-start | bytes 141320 | tf_op jit(solution)/shard_map/ppermute | solution.py:32
  136.0 4.3 %collective-permute-start.32 = (f32[2,46,128]{2,1,0:T(8,128)S(1)}, f32[2,46,128]{2,1,0:T(8,128)}, u32[]{:S(2)}, u32[]{:S(2)}) collective-permute-start(f32[2,46,128]{2,1,0:T(8,128)S(1)} %collective-permute-done.31), channel_id=1, source_target_pairs={{0,16},{16,0},{4,20},{20,4},{8,24},{24,8},{12,28},{28,12},{1,17},{... | collective-permute-start | bytes 141320 | tf_op jit(solution)/shard_map/ppermute | solution.py:19
  137.8 9.2 %collective-permute-start.28 = (f32[2,46,8,1]{3,2,1,0:T(8,128)}, f32[2,46,8,1]{3,2,1,0:T(8,128)S(1)}, u32[]{:S(2)}, u32[]{:S(2)}) collective-permute-start(f32[2,46,8,1]{3,2,1,0:T(8,128)} %get-tuple-element.146), channel_id=1, source_target_pairs={{4,0},{8,4},{12,8},{16,12},{20,16},{24,20},{28,24},{0,28},{5,1},{9... | collective-permute-start | bytes 8840 | tf_op jit(solution)/shard_map/ppermute | solution.py:32
  138.0 11.6 %collective-permute-start.29 = (f32[2,46,8,1]{3,2,1,0:T(8,128)}, f32[2,46,8,1]{3,2,1,0:T(8,128)}, u32[]{:S(2)}, u32[]{:S(2)}) collective-permute-start(f32[2,46,8,1]{3,2,1,0:T(8,128)} %get-tuple-element.147), channel_id=1, source_target_pairs={{0,4},{4,8},{8,12},{12,16},{16,20},{20,24},{24,28},{28,0},{1,5},{5... | collective-permute-start | bytes 8840 | tf_op jit(solution)/shard_map/ppermute | solution.py:30
  (144 other events, 402.8 us)
where the time goes:
time: 172 us; the launch traced here: 170 us
  starting transfers between devices  48.3 us (28%)
  waiting for transfers between devices  43.1 us (25%)
  local copies, waits for them, and re-layouts  39.1 us (23%)
  other arithmetic  37.6 us (22%)
  between operations  2.13 us (1%)
    ppermute x10, starting transfers between devices, padded(): lax.ppermute(tail, axis, [(i, (i + 1) % count) for i in range(ends)])  26.1 us
    ppermute x10, waiting for transfers between devices, padded(): lax.ppermute(head, axis, [((i + 1) % count, i) for i in range(ends)])  25.8 us
    unnamed x309, local copies, waits for them, and re-layouts  23.1 us
    mul x22, other arithmetic, tridiagonal(): ratio_list[level_index] * solved_level  15.9 us
    ppermute x15, starting transfers between devices, partner(): return lax.ppermute(block, axis, route)  12 us
    ppermute x15, waiting for transfers between devices, partner(): return lax.ppermute(block, axis, route)  10.3 us
    ppermute x10, starting transfers between devices, padded(): lax.ppermute(head, axis, [((i + 1) % count, i) for i in range(ends)])  10.2 us
    sub x4, other arithmetic, advance(): return scalar_quantities - (flux_east - flux_west + flux_north - flux_south)  7.29 us
  transfers between devices with their start and end apart: 35, of which 16 were waited for; matrix products, arithmetic and copies ran while one was open for 22% of the time, Pallas kernels for 0%

commit v1 on v0

v1 whole, which is shorter than its diff:
```python
import functools

import jax
import jax.numpy as jnp
from jax import lax
from jax.experimental import pallas as pl
from jax.experimental.pallas import tpu as pltpu
from jax.sharding import PartitionSpec as P

PASSES = 4
DIFFUSE = 0.05
MESH = pl.DeviceIdType.MESH
F32 = jnp.float32


def tracer_kernel(
    nlon, nlat, depth,
    th, sa, zo, me, vd, fr, ind, dep, out_t, out_s,
    fields, maps, c, acc, ef, nf, coef, dv, upp, low, ip, mm, qq, res,
    lon_out, lon_w, lon_e, n_out, s_out, n_in, s_in,
    in_sem, send_sem, recv_sem, out_sem,
):
    padded = -(-depth // 8) * 8
    rows = 8 * depth
    lon = lax.axis_index("lon")
    lat = lax.axis_index("lat")
    is_top = lat == nlat - 1
    east = lax.rem(lon + 1, nlon)
    west = lax.rem(lon + nlon - 1, nlon)
    mirror = nlon - 1 - lon

    barrier = pltpu.get_barrier_semaphore()

    def greet(i, j):
        pl.semaphore_signal(barrier, inc=1, device_id={"lon": i, "lat": j}, device_id_type=MESH)

    greet(east, lat)
    greet(west, lat)

    @pl.when(is_top)
    def _():
        greet(mirror, lat)

    @pl.when(jnp.logical_not(is_top))
    def _():
        greet(lon, lat + 1)

    @pl.when(lat > 0)
    def _():
        greet(lon, lat - 1)

    loads = [
        pltpu.make_async_copy(ind, maps.at[0], in_sem.at[0]),
        pltpu.make_async_copy(dep, maps.at[1], in_sem.at[1]),
    ]
    for f, ref in enumerate((fr, zo, me, th, sa, vd)):
        loads.append(pltpu.make_async_copy(ref, fields.at[f], in_sem.at[2 + f]))
    for load in loads:
        load.start()

    lane = lax.broadcasted_iota(jnp.int32, (8, 128), 1)
    sub = lax.broadcasted_iota(jnp.int32, (8, 128), 0)
    pair = lax.shift_right_logical(lane, 1)
    even = (lane & 1) == 0
    first, last = lane == 0, lane == 127
    bottom_row, top_row = sub == 0, sub == 7
    hinge = jnp.logical_and(top_row, is_top)
    turned = jnp.where(is_top, 127 - lane, lane)
    zero = jnp.zeros((8, 128), F32)

    def at(k):
        return pl.ds(pl.multiple_of(k * 8, 8), 8)

    def loop(count, body, init):
        return lax.fori_loop(0, count, body, init, unroll=count)

    def pack(x, k, packed):
        return jnp.where(pair == k, pltpu.roll(x, 2 * k + 1, 1), packed)

    def merge(from_west, from_east):
        return jnp.where(even, pltpu.roll(from_east, 127, 1), pltpu.roll(from_west, 1, 1))

    def unpack(merged, k):
        return pltpu.roll(merged, 127 - 2 * k, 1)

    def spread(ref, r, row):
        return jnp.broadcast_to(ref[r, pl.ds(row, 1), :], (8, 128))

    def turn(x):
        return jnp.take_along_axis(x, turned, axis=1, mode="promise_in_bounds")

    def stage_rows(r, ref, base, slot):
        for j in range(padded // 8):
            place = pl.ds(8 + slot * padded + 8 * j, 8)
            s_out[r, place, :] = ref[pl.ds(base + 64 * j, 8, stride=8), :]
            n_out[r, place, :] = turn(ref[pl.ds(base + 64 * j + 7, 8, stride=8), :])

    def remote(src, dst, r, way, i, j):
        return pltpu.make_async_remote_copy(
            src_ref=src, dst_ref=dst, send_sem=send_sem.at[r, way], recv_sem=recv_sem.at[r, way],
            device_id={"lon": i, "lat": j}, device_id_type=MESH,
        )

    def span(r):
        if r == 0:
            return pl.ds(0, 24), pl.ds(0, 8 + 3 * padded)
        return pl.ds(0, 16), pl.ds(8, 2 * padded)

    def to_east(r):
        s = span(r)[0]
        return remote(lon_out.at[r, s], lon_w.at[r, s], r, 0, east, lat)

    def to_west(r):
        s = span(r)[0]
        return remote(lon_out.at[r, s], lon_e.at[r, s], r, 1, west, lat)

    def to_north(r):
        s = span(r)[1]
        return remote(n_out.at[r, s], s_in.at[r, s], r, 3, lon, lat + 1)

    def to_mirror(r):
        s = span(r)[1]
        return pltpu.make_async_remote_copy(
            src_ref=n_out.at[r, s], dst_ref=n_in.at[r, s], send_sem=send_sem.at[r, 3],
            recv_sem=recv_sem.at[r, 2], device_id={"lon": mirror, "lat": lat}, device_id_type=MESH,
        )

    def to_south(r):
        s = span(r)[1]
        return remote(s_out.at[r, s], n_in.at[r, s], r, 2, lon, lat - 1)

    def send_lat(r):
        @pl.when(is_top)
        def _():
            to_mirror(r).start()

        @pl.when(jnp.logical_not(is_top))
        def _():
            to_north(r).start()

        @pl.when(lat > 0)
        def _():
            to_south(r).start()

    def send_lon(r):
        to_east(r).start()
        to_west(r).start()

    def wait_recv(r):
        to_east(r).wait_recv()
        to_west(r).wait_recv()
        to_south(r).wait_recv()

        @pl.when(lat > 0)
        def _():
            to_north(r).wait_recv()

    def wait_send(r):
        to_east(r).wait_send()
        to_west(r).wait_send()
        to_mirror(r).wait_send()

        @pl.when(lat > 0)
        def _():
            to_south(r).wait_send()

    for t in range(2):
        c[pl.ds(t * 8 * padded + rows, 8 * padded - rows), :] = jnp.zeros((8 * padded - rows, 128), F32)
    nf[pl.ds(rows, 8 * padded - rows), :] = jnp.zeros((8 * padded - rows, 128), F32)

    @pl.when(lat == 0)
    def _():
        s_in[...] = jnp.zeros(s_in.shape, F32)

    for load in loads[:7]:
        load.wait()
    count = jnp.where(maps[0] == 1, maps[1], 0).astype(F32)

    def prepare(k, packs):
        pt, ps, pe = packs
        drag = 1.0 / (1.0 + fields[0, at(k), :])
        e = fields[1, at(k), :] * drag
        ef[at(k), :] = e
        nf[at(k), :] = fields[2, at(k), :] * drag
        wet = k.astype(F32) < count
        x = jnp.where(wet, fields[3, at(k), :], 0.0)
        y = jnp.where(wet, fields[4, at(k), :], 0.0)
        c[at(k), :] = x
        c[at(padded + k), :] = y
        return pack(x, k, pt), pack(y, k, ps), pack(e, k, pe)

    pt, ps, pe = loop(depth, prepare, (zero, zero, zero))
    lon_out[0, 0:8, :] = pt
    lon_out[0, 8:16, :] = ps
    lon_out[0, 16:24, :] = pack(count, depth, pe)
    n_out[0, 0:8, :] = turn(jnp.broadcast_to(count[7:8, :], (8, 128)))
    s_out[0, 0:8, :] = jnp.broadcast_to(count[0:1, :], (8, 128))
    for t in range(2):
        stage_rows(0, c, t * 8 * padded, t)
    stage_rows(0, nf, 0, 2)
    pl.semaphore_wait(barrier, 3 + jnp.where(lat > 0, 1, 0))
    send_lat(0)
    send_lon(0)
    wait_recv(0)

    edges = merge(lon_w[0, 16:24, :], lon_e[0, 16:24, :])
    rim = unpack(edges, depth)
    least_w = jnp.minimum(count, jnp.where(first, rim, pltpu.roll(count, 1, 1)))
    least_e = jnp.minimum(count, jnp.where(last, rim, pltpu.roll(count, 127, 1)))
    least_s = jnp.minimum(count, jnp.where(bottom_row, s_in[0, 0:8, :], pltpu.roll(count, 1, 0)))
    least_n = jnp.minimum(count, jnp.where(top_row, n_in[0, 0:8, :], pltpu.roll(count, 7, 0)))

    def faces(k, carry):
        level = k.astype(F32)
        e, n = ef[at(k), :], nf[at(k), :]
        w = jnp.where(first, unpack(edges, k), pltpu.roll(e, 1, 1))
        s = jnp.where(bottom_row, spread(s_in, 0, 8 + 2 * padded + k), pltpu.roll(n, 1, 0))
        n = jnp.where(hinge, 0.5 * (n - spread(n_in, 0, 8 + 2 * padded + k)), n)
        oe, ow, on, os = level < least_e, level < least_w, level < least_n, level < least_s
        fe, fw = jnp.where(oe, e, 0.0), jnp.where(ow, w, 0.0)
        fn, fs = jnp.where(on, n, 0.0), jnp.where(os, s, 0.0)
        de, dw = jnp.where(oe, DIFFUSE, 0.0), jnp.where(ow, DIFFUSE, 0.0)
        dn, ds = jnp.where(on, DIFFUSE, 0.0), jnp.where(os, DIFFUSE, 0.0)
        ne, pw = de - jnp.minimum(fe, 0.0), jnp.maximum(fw, 0.0) + dw
        nn, p_s = dn - jnp.minimum(fn, 0.0), jnp.maximum(fs, 0.0) + ds
        coef[0, at(k), :] = 1.0 - ((fe + ne) + (pw - fw) + (fn + nn) + (p_s - fs))
        coef[1, at(k), :] = jnp.where(last, 0.0, ne)
        coef[2, at(k), :] = jnp.where(first, 0.0, pw)
        coef[3, at(k), :] = jnp.where(top_row, 0.0, nn)
        coef[4, at(k), :] = jnp.where(bottom_row, 0.0, p_s)
        coef[5, at(k), :] = jnp.where(first, pw, jnp.where(last, ne, 0.0))
        coef[6, at(k), :] = jnp.where(bottom_row, p_s, jnp.where(top_row, nn, 0.0))
        dv[at(k), :] = fe - fw + fn - fs
        return carry

    loop(depth, faces, 0)

    def interior():
        def body(k, carry):
            a = [coef[i, at(k), :] for i in range(5)]
            for t in range(2):
                x = c[at(t * padded + k), :]
                acc[at(t * depth + k), :] = (
                    (a[0] * x + a[1] * pltpu.roll(x, 127, 1))
                    + (a[2] * pltpu.roll(x, 1, 1) + a[3] * pltpu.roll(x, 7, 0))
                    + a[4] * pltpu.roll(x, 1, 0)
                )
            return carry

        loop(depth, body, 0)

    def completed(r, t, k, merged):
        rims = jnp.where(
            bottom_row, spread(s_in, r, 8 + t * padded + k), spread(n_in, r, 8 + t * padded + k)
        )
        return acc[at(t * depth + k), :] + (
            coef[5, at(k), :] * unpack(merged, k) + coef[6, at(k), :] * rims
        )

    def merged_of(r):
        return [
            merge(lon_w[r, 8 * t:8 * t + 8, :], lon_e[r, 8 * t:8 * t + 8, :]) for t in range(2)
        ]

    def column_bands():
        loads[7].wait()
        upp[at(0), :] = zero
        low[at(0), :] = zero
        upp[at(depth), :] = zero
        low[at(depth), :] = zero

        def deeper(i, total):
            k = depth - 1 - i
            total = total + dv[at(k), :]
            flow = -float(PASSES) * total
            mixing = jnp.where(k.astype(F32) < count, fields[5, at(k - 1), :], 0.0)
            upp[at(k), :] = jnp.maximum(flow, 0.0) + mixing
            low[at(k), :] = mixing - jnp.minimum(flow, 0.0)
            return total

        loop(depth - 1, deeper, zero)

        def pivots(k, q):
            l, u = low[at(k), :], upp[at(k + 1), :]
            inv = 1.0 / (1.0 + low[at(k + 1), :] + upp[at(k), :] - l * q)
            q = u * inv
            ip[at(k), :] = inv
            mm[at(k), :] = l * inv
            qq[at(k), :] = q
            return q

        loop(depth, pivots, zero)

    interior()
    for r in range(PASSES - 1):
        merged = merged_of(r)

        def complete(k, packs):
            new = []
            for t in range(2):
                x = completed(r, t, k, merged[t])
                c[at(t * padded + k), :] = x
                new.append(pack(x, k, packs[t]))
            return tuple(new)

        packs = loop(depth, complete, (zero, zero))
        lon_out[r + 1, 0:8, :] = packs[0]
        lon_out[r + 1, 8:16, :] = packs[1]
        for t in range(2):
            stage_rows(r + 1, c, t * 8 * padded, t)
        send_lat(r + 1)
        send_lon(r + 1)
        interior()
        if r == 0:
            column_bands()
        wait_recv(r + 1)

    merged = merged_of(PASSES - 1)

    def forward(k, values):
        new = []
        for t in range(2):
            x = completed(PASSES - 1, t, k, merged[t])
            v = x * ip[at(k), :] + mm[at(k), :] * values[t]
            res[at(t * depth + k), :] = v
            new.append(v)
        return tuple(new)

    values = loop(depth, forward, (zero, zero))

    half = depth // 2

    def backward(start):
        def body(i, values):
            k = start - i
            q = qq[at(k), :]
            new = []
            for t in range(2):
                x = res[at(t * depth + k), :] + q * values[t]
                res[at(t * depth + k), :] = x
                new.append(x)
            return tuple(new)

        return body

    stores = []

    def store(part, begin, size):
        for t, ref in enumerate((out_t, out_s)):
            copy = pltpu.make_async_copy(
                res.at[pl.ds(t * rows + begin * 8, size * 8)],
                ref.at[pl.ds(begin * 8, size * 8)],
                out_sem.at[part, t],
            )
            copy.start()
            stores.append(copy)

    values = loop(depth - half, backward(depth - 1), (zero, zero))
    store(0, half, depth - half)
    loop(half, backward(half - 1), values)
    store(1, 0, half)
    for r in range(PASSES):
        wait_send(r)
    for copy in stores:
        copy.wait()


def solution(mesh):
    nlon, nlat = mesh.shape["lon"], mesh.shape["lat"]
    cube, plane = P(None, "lat", "lon"), P("lat", "lon")

    def shards(*args):
        depth = args[0].shape[0]
        padded = -(-depth // 8) * 8
        rows = 8 * depth
        flat = [a.reshape(rows, 128) for a in args[:6]] + list(args[6:])
        edge_rows = 8 + 3 * padded
        vmem = pltpu.VMEM
        scratch = [
            vmem((6, rows, 128), F32), vmem((2, 8, 128), jnp.int32),
            vmem((16 * padded, 128), F32), vmem((2 * rows, 128), F32),
            vmem((rows, 128), F32), vmem((8 * padded, 128), F32),
            vmem((7, rows, 128), F32), vmem((rows, 128), F32),
            vmem((rows + 8, 128), F32), vmem((rows + 8, 128), F32),
            vmem((rows, 128), F32), vmem((rows, 128), F32), vmem((rows, 128), F32),
            vmem((2 * rows, 128), F32),
        ]
        scratch += [vmem((PASSES, 24, 128), F32) for _ in range(3)]
        scratch += [vmem((PASSES, edge_rows, 128), F32) for _ in range(4)]
        scratch += [
            pltpu.SemaphoreType.DMA((8,)), pltpu.SemaphoreType.DMA((PASSES, 4)),
            pltpu.SemaphoreType.DMA((PASSES, 4)), pltpu.SemaphoreType.DMA((2, 2)),
        ]
        outs = pl.pallas_call(
            functools.partial(tracer_kernel, nlon, nlat, depth),
            out_shape=[jax.ShapeDtypeStruct((rows, 128), F32)] * 2,
            in_specs=[pl.BlockSpec(memory_space=pl.ANY)] * 8,
            out_specs=[pl.BlockSpec(memory_space=pl.ANY)] * 2,
            scratch_shapes=scratch,
            compiler_params=pltpu.CompilerParams(
                collective_id=0, has_side_effects=True, vmem_limit_bytes=32 * 1024 * 1024
            ),
            cost_estimate=pl.CostEstimate(flops=20000000, bytes_accessed=1600000, transcendentals=0),
            name="tracer_step",
        )(*flat)
        return tuple(o.reshape(depth, 8, 128) for o in outs)

    return jax.shard_map(
        shards, mesh=mesh, in_specs=(cube,) * 6 + (plane,) * 2, out_specs=(cube, cube), check_vma=False
    )
```

time: 172 us -> 30.4 us (0.18)
  starting transfers between devices: 48.3 us -> 0 us
  waiting for transfers between devices: 43.1 us -> 0 us
  other arithmetic: 37.6 us -> 0 us
  local copies, waits for them, and re-layouts: 39.1 us -> 7.58 us
  Pallas kernels: 0 us -> 21.8 us
    ppermute x35 -> x0, starting transfers between devices: 48.3 us -> none  [the longest x10 26.1 us: padded(): lax.ppermute(tail, axis, [(i, (i + 1) % count) for i in range(ends)])]
    ppermute x35 -> x0, waiting for transfers between devices: 43.1 us -> none  [the longest x10 25.8 us: padded(): lax.ppermute(head, axis, [((i + 1) % count, i) for i in range(ends)])]
    pallas_call x0 -> x1, Pallas kernels: none -> 21.8 us  [shards(): pl.pallas_call(functools.partial(tracer_kernel, nlon, nlat, depth), out_s...]
    mul x28 -> x0, other arithmetic: 17 us -> none  [the longest x22 15.9 us: tridiagonal(): ratio_list[level_index] * solved_level]
    unnamed x309 -> x18, local copies, waits for them, and re-layouts: 23.1 us -> 7.58 us
    slice x18 -> x0, local copies, waits for them, and re-layouts: 9.83 us -> none  [the longest x10 7.12 us: padded(): head = lax.slice_in_dim(cells, 0, width, axis=dim)]
    sub x6 -> x0, other arithmetic: 7.36 us -> none  [the longest x4 7.29 us: advance(): return scalar_quantities - (flux_east - flux_west + flux_north - flux_south)]
    rev x6 -> x0, local copies, waits for them, and re-layouts: 3.58 us -> none  [the longest x5 3.57 us: mirrored(): return swapped[:, :, ::-1]]
  transfers between devices with their start and end apart: 35 -> 0, of which waited for: 16 -> 0; matrix products, arithmetic and copies ran while one was open for 22% -> 0% of each run, Pallas kernels for 0% -> 0%
where the time goes in v1:
time: 30.4 us; the launch traced here: 30.1 us
  Pallas kernels  21.8 us (72%)
  local copies, waits for them, and re-layouts  7.58 us (25%)
  between operations  0.66 us (2%)
    pallas_call x1, Pallas kernels, shards(): pl.pallas_call(functools.partial(tracer_kernel, nlon, nlat, depth), out_s...  21.8 us
    unnamed x18, local copies, waits for them, and re-layouts  7.58 us

profile of v1, /device:TPU:0, one launch (start us, length us, event | category | flops | bytes accessed | tf_op | source)
XLA Modules:
  0.0 30.1 jit_solution(4797367524802567982)
XLA Ops:
  0.6 0.0 copy-start.7
  0.6 0.0 copy-start.6
  0.7 0.7 %copy-done.7 = s32[8,128]{1,0:T(8,128)S(1)} copy-done((s32[8,128]{1,0:T(8,128)S(1)}, s32[8,128]{1,0:T(8,128)}, u32[]{:S(2)}) %copy-start.7) | copy-done | bytes 4120
  1.3 0.0 copy-done.6
  1.3 0.0 copy-start
  1.3 0.9 %copy-done = f32[46,8,128]{2,1,0:T(8,128)S(1)} copy-done((f32[46,8,128]{2,1,0:T(8,128)S(1)}, f32[46,8,128]{2,1,0:T(8,128)}, u32[]{:S(2)}) %copy-start) | copy-done | bytes 188440
  2.3 0.0 copy-start.1
  2.3 0.9 %copy-done.1 = f32[46,8,128]{2,1,0:T(8,128)S(1)} copy-done((f32[46,8,128]{2,1,0:T(8,128)S(1)}, f32[46,8,128]{2,1,0:T(8,128)}, u32[]{:S(2)}) %copy-start.1) | copy-done | bytes 188440
  3.2 0.0 copy-start.2
  3.2 0.9 %copy-done.2 = f32[46,8,128]{2,1,0:T(8,128)S(1)} copy-done((f32[46,8,128]{2,1,0:T(8,128)S(1)}, f32[46,8,128]{2,1,0:T(8,128)}, u32[]{:S(2)}) %copy-start.2) | copy-done | bytes 188440
  4.1 0.0 copy-start.3
  4.1 0.9 %copy-done.3 = f32[46,8,128]{2,1,0:T(8,128)S(1)} copy-done((f32[46,8,128]{2,1,0:T(8,128)S(1)}, f32[46,8,128]{2,1,0:T(8,128)}, u32[]{:S(2)}) %copy-start.3) | copy-done | bytes 188440
  5.0 0.0 copy-start.4
  5.0 0.9 %copy-done.4 = f32[46,8,128]{2,1,0:T(8,128)S(1)} copy-done((f32[46,8,128]{2,1,0:T(8,128)S(1)}, f32[46,8,128]{2,1,0:T(8,128)}, u32[]{:S(2)}) %copy-start.4) | copy-done | bytes 188440
  6.0 0.0 copy-start.5
  6.0 0.9 %copy-done.5 = f32[46,8,128]{2,1,0:T(8,128)S(1)} copy-done((f32[46,8,128]{2,1,0:T(8,128)S(1)}, f32[46,8,128]{2,1,0:T(8,128)}, u32[]{:S(2)}) %copy-start.5) | copy-done | bytes 188440
  6.9 21.8 %tracer_step.1 = (f32[368,128]{1,0:T(8,128)S(1)}, f32[368,128]{1,0:T(8,128)S(1)}) custom-call(f32[368,128]{1,0:T(8,128)S(1)} %bitcast.8, f32[368,128]{1,0:T(8,128)S(1)} %bitcast.9, f32[368,128]{1,0:T(8,128)S(1)} %bitcast.10, f32[368,128]{1,0:T(8,128)S(1)} %bitcast.11, f32[368,128]{1,0:T(8,128)S(1)} %bitcast.12, f32[368,128]{1,0:T(8,128)S(1)} %bitcast.13, ...), custom_call_target="tpu_custom_call" | custom-call | flops 20000000 | bytes 1600000 | tf_op jit(solution)/shard_map/tracer_step/pallas_call | solution.py:394
  28.7 0.7 %copy.12 = f32[46,8,128]{2,1,0:T(8,128)} copy(f32[46,8,128]{2,1,0:T(8,128)S(1)} %bitcast.15) | data formatting | bytes 376832
  29.4 0.7 %copy.13 = f32[46,8,128]{2,1,0:T(8,128)} copy(f32[46,8,128]{2,1,0:T(8,128)S(1)} %bitcast.14) | data formatting | bytes 376832
Async XLA Ops:
  0.6 0.7 %copy-start.7 = (s32[8,128]{1,0:T(8,128)S(1)}, s32[8,128]{1,0:T(8,128)}, u32[]{:S(2)}) copy-start(s32[8,128]{1,0:T(8,128)} %dep.1) | copy-start | bytes 12292
  0.6 0.7 %copy-start.6 = (s32[8,128]{1,0:T(8,128)S(1)}, s32[8,128]{1,0:T(8,128)}, u32[]{:S(2)}) copy-start(s32[8,128]{1,0:T(8,128)} %ind.1) | copy-start | bytes 12292
  1.3 0.9 %copy-start = (f32[46,8,128]{2,1,0:T(8,128)S(1)}, f32[46,8,128]{2,1,0:T(8,128)}, u32[]{:S(2)}) copy-start(f32[46,8,128]{2,1,0:T(8,128)} %param.8) | copy-start | bytes 565252
  2.3 0.9 %copy-start.1 = (f32[46,8,128]{2,1,0:T(8,128)S(1)}, f32[46,8,128]{2,1,0:T(8,128)}, u32[]{:S(2)}) copy-start(f32[46,8,128]{2,1,0:T(8,128)} %param.9) | copy-start | bytes 565252
  3.2 0.9 %copy-start.2 = (f32[46,8,128]{2,1,0:T(8,128)S(1)}, f32[46,8,128]{2,1,0:T(8,128)}, u32[]{:S(2)}) copy-start(f32[46,8,128]{2,1,0:T(8,128)} %param.10) | copy-start | bytes 565252
  4.1 0.9 %copy-start.3 = (f32[46,8,128]{2,1,0:T(8,128)S(1)}, f32[46,8,128]{2,1,0:T(8,128)}, u32[]{:S(2)}) copy-start(f32[46,8,128]{2,1,0:T(8,128)} %param.11) | copy-start | bytes 565252
  5.0 0.9 %copy-start.4 = (f32[46,8,128]{2,1,0:T(8,128)S(1)}, f32[46,8,128]{2,1,0:T(8,128)}, u32[]{:S(2)}) copy-start(f32[46,8,128]{2,1,0:T(8,128)} %param.12) | copy-start | bytes 565252
  6.0 0.9 %copy-start.5 = (f32[46,8,128]{2,1,0:T(8,128)S(1)}, f32[46,8,128]{2,1,0:T(8,128)}, u32[]{:S(2)}) copy-start(f32[46,8,128]{2,1,0:T(8,128)} %param.13) | copy-start | bytes 565252

commit v2 on v1

v2 whole, which is shorter than its diff:
```python
import functools

import jax
import jax.numpy as jnp
from jax import lax
from jax.experimental import pallas as pl
from jax.experimental.pallas import tpu as pltpu
from jax.sharding import PartitionSpec as P

PASSES = 4
DIFFUSE = 0.05
MESH = pl.DeviceIdType.MESH
F32 = jnp.float32


def tracer_kernel(
    nlon, nlat, depth,
    th, sa, zo, me, vd, fr, ind, dep, out_t, out_s,
    fields, maps, c, acc, ef, nf, coef, dv, upp, low, ip, mm, qq, res,
    lon_out, lon_w, lon_e, n_out, s_out, n_in, s_in,
    in_sem, send_sem, recv_sem,
):
    padded = -(-depth // 8) * 8
    rows = 8 * depth
    lon = lax.axis_index("lon")
    lat = lax.axis_index("lat")
    is_top = lat == nlat - 1
    east = lax.rem(lon + 1, nlon)
    west = lax.rem(lon + nlon - 1, nlon)
    mirror = nlon - 1 - lon

    barrier = pltpu.get_barrier_semaphore()

    def greet(i, j):
        pl.semaphore_signal(barrier, inc=1, device_id={"lon": i, "lat": j}, device_id_type=MESH)

    greet(east, lat)
    greet(west, lat)

    @pl.when(is_top)
    def _():
        greet(mirror, lat)

    @pl.when(jnp.logical_not(is_top))
    def _():
        greet(lon, lat + 1)

    @pl.when(lat > 0)
    def _():
        greet(lon, lat - 1)

    loads = [
        pltpu.make_async_copy(ind, maps.at[0], in_sem.at[0]),
        pltpu.make_async_copy(dep, maps.at[1], in_sem.at[1]),
    ]
    for f, ref in enumerate((fr, zo, me, th, sa, vd)):
        loads.append(pltpu.make_async_copy(ref, fields.at[f], in_sem.at[2 + f]))
    for load in loads:
        load.start()

    lane = lax.broadcasted_iota(jnp.int32, (8, 128), 1)
    sub = lax.broadcasted_iota(jnp.int32, (8, 128), 0)
    pair = lax.shift_right_logical(lane, 1)
    even = (lane & 1) == 0
    first, last = lane == 0, lane == 127
    bottom_row, top_row = sub == 0, sub == 7
    hinge = jnp.logical_and(top_row, is_top)
    turned = jnp.where(is_top, 127 - lane, lane)
    zero = jnp.zeros((8, 128), F32)

    def at(k):
        return pl.ds(pl.multiple_of(k * 8, 8), 8)

    def loop(count, body, init):
        return lax.fori_loop(0, count, body, init, unroll=count)

    def pack(x, k, packed):
        return jnp.where(pair == k, pltpu.roll(x, 2 * k + 1, 1), packed)

    def merge(from_west, from_east):
        return jnp.where(even, pltpu.roll(from_east, 127, 1), pltpu.roll(from_west, 1, 1))

    def unpack(merged, k):
        return pltpu.roll(merged, 127 - 2 * k, 1)

    def spread(ref, r, row):
        return jnp.broadcast_to(ref[r, pl.ds(row, 1), :], (8, 128))

    def turn(x):
        return jnp.take_along_axis(x, turned, axis=1, mode="promise_in_bounds")

    def stage_rows(r, ref, base, row):
        for j in range(padded // 8):
            place = pl.ds(row + 8 * j, 8)
            s_out[r, place, :] = ref[pl.ds(base + 64 * j, 8, stride=8), :]
            n_out[r, place, :] = turn(ref[pl.ds(base + 64 * j + 7, 8, stride=8), :])

    def copy_to(src, dst, r, g, way_out, way_in, i, j):
        return pltpu.make_async_remote_copy(
            src_ref=src, dst_ref=dst, send_sem=send_sem.at[r, g, way_out],
            recv_sem=recv_sem.at[r, g, way_in], device_id={"lon": i, "lat": j}, device_id_type=MESH,
        )

    def to_east(r, g):
        s = pl.ds(8 * g, 8)
        return copy_to(lon_out.at[r, s], lon_w.at[r, s], r, g, 0, 0, east, lat)

    def to_west(r, g):
        s = pl.ds(8 * g, 8)
        return copy_to(lon_out.at[r, s], lon_e.at[r, s], r, g, 1, 1, west, lat)

    def rows_of(g):
        return pl.ds(g * padded, padded + 8 if g == 2 else padded)

    def to_north(r, g):
        s = rows_of(g)
        return copy_to(n_out.at[r, s], s_in.at[r, s], r, g, 3, 3, lon, lat + 1)

    def to_mirror(r, g):
        s = rows_of(g)
        return copy_to(n_out.at[r, s], n_in.at[r, s], r, g, 3, 2, mirror, lat)

    def to_south(r, g):
        s = pl.ds(2 * padded, 8) if g == 2 else rows_of(g)
        return copy_to(s_out.at[r, s], n_in.at[r, s], r, g, 2, 2, lon, lat - 1)

    def send(r, g):
        @pl.when(is_top)
        def _():
            to_mirror(r, g).start()

        @pl.when(jnp.logical_not(is_top))
        def _():
            to_north(r, g).start()

        @pl.when(lat > 0)
        def _():
            to_south(r, g).start()

        to_east(r, g).start()
        to_west(r, g).start()

    def wait_recv(r, g):
        to_east(r, g).wait_recv()
        to_west(r, g).wait_recv()
        if g == 2:
            @pl.when(is_top)
            def _():
                to_mirror(r, g).wait_recv()

            @pl.when(jnp.logical_not(is_top))
            def _():
                to_south(r, g).wait_recv()
        else:
            to_south(r, g).wait_recv()

        @pl.when(lat > 0)
        def _():
            to_north(r, g).wait_recv()

    def wait_send(r, g):
        to_east(r, g).wait_send()
        to_west(r, g).wait_send()
        to_mirror(r, g).wait_send()

        @pl.when(lat > 0)
        def _():
            to_south(r, g).wait_send()

    for t in range(2):
        c[pl.ds(t * 8 * padded + rows, 8 * padded - rows), :] = jnp.zeros((8 * padded - rows, 128), F32)
    nf[pl.ds(rows, 8 * padded - rows), :] = jnp.zeros((8 * padded - rows, 128), F32)

    @pl.when(lat == 0)
    def _():
        s_in[...] = jnp.zeros(s_in.shape, F32)

    @pl.when(jnp.logical_not(is_top))
    def _():
        n_in[0, pl.ds(2 * padded + 8, padded), :] = jnp.zeros((padded, 128), F32)

    for load in loads[:5]:
        load.wait()
    count = jnp.where(maps[0] == 1, maps[1], 0).astype(F32)

    def flows(k, packed):
        drag = 1.0 / (1.0 + fields[0, at(k), :])
        e = fields[1, at(k), :] * drag
        ef[at(k), :] = e
        nf[at(k), :] = fields[2, at(k), :] * drag
        return pack(e, k, packed)

    lon_out[0, 16:24, :] = pack(count, depth, loop(depth, flows, zero))
    n_out[0, pl.ds(2 * padded, 8), :] = turn(jnp.broadcast_to(count[7:8, :], (8, 128)))
    s_out[0, pl.ds(2 * padded, 8), :] = jnp.broadcast_to(count[0:1, :], (8, 128))
    stage_rows(0, nf, 0, 2 * padded + 8)
    pl.semaphore_wait(barrier, 3 + jnp.where(lat > 0, 1, 0))
    send(0, 2)
    for t in range(2):
        loads[5 + t].wait()

        def masked(k, packed):
            x = jnp.where(k.astype(F32) < count, fields[3 + t, at(k), :], 0.0)
            c[at(t * padded + k), :] = x
            return pack(x, k, packed)

        lon_out[0, 8 * t:8 * t + 8, :] = loop(depth, masked, zero)
        stage_rows(0, c, t * 8 * padded, t * padded)
        send(0, t)
    wait_recv(0, 2)

    edges = merge(lon_w[0, 16:24, :], lon_e[0, 16:24, :])
    rim = unpack(edges, depth)
    least_w = jnp.minimum(count, jnp.where(first, rim, pltpu.roll(count, 1, 1)))
    least_e = jnp.minimum(count, jnp.where(last, rim, pltpu.roll(count, 127, 1)))
    least_s = jnp.minimum(count, jnp.where(bottom_row, s_in[0, pl.ds(2 * padded, 8), :], pltpu.roll(count, 1, 0)))
    least_n = jnp.minimum(count, jnp.where(top_row, n_in[0, pl.ds(2 * padded, 8), :], pltpu.roll(count, 7, 0)))

    def faces(k, carry):
        level = k.astype(F32)
        e, n = ef[at(k), :], nf[at(k), :]
        w = jnp.where(first, unpack(edges, k), pltpu.roll(e, 1, 1))
        s = jnp.where(bottom_row, spread(s_in, 0, 2 * padded + 8 + k), pltpu.roll(n, 1, 0))
        n = jnp.where(hinge, 0.5 * (n - spread(n_in, 0, 2 * padded + 8 + k)), n)
        oe, ow, on, os = level < least_e, level < least_w, level < least_n, level < least_s
        fe, fw = jnp.where(oe, e, 0.0), jnp.where(ow, w, 0.0)
        fn, fs = jnp.where(on, n, 0.0), jnp.where(os, s, 0.0)
        de, dw = jnp.where(oe, DIFFUSE, 0.0), jnp.where(ow, DIFFUSE, 0.0)
        dn, ds = jnp.where(on, DIFFUSE, 0.0), jnp.where(os, DIFFUSE, 0.0)
        ne, pw = de - jnp.minimum(fe, 0.0), jnp.maximum(fw, 0.0) + dw
        nn, p_s = dn - jnp.minimum(fn, 0.0), jnp.maximum(fs, 0.0) + ds
        coef[0, at(k), :] = 1.0 - ((fe + ne) + (pw - fw) + (fn + nn) + (p_s - fs))
        coef[1, at(k), :] = jnp.where(last, 0.0, ne)
        coef[2, at(k), :] = jnp.where(first, 0.0, pw)
        coef[3, at(k), :] = jnp.where(top_row, 0.0, nn)
        coef[4, at(k), :] = jnp.where(bottom_row, 0.0, p_s)
        coef[5, at(k), :] = jnp.where(first, pw, jnp.where(last, ne, 0.0))
        coef[6, at(k), :] = jnp.where(bottom_row, p_s, jnp.where(top_row, nn, 0.0))
        dv[at(k), :] = fe - fw + fn - fs
        return carry

    loop(depth, faces, 0)

    def interior(t):
        def body(k, carry):
            a = [coef[i, at(k), :] for i in range(5)]
            x = c[at(t * padded + k), :]
            acc[at(t * depth + k), :] = (
                (a[0] * x + a[1] * pltpu.roll(x, 127, 1))
                + (a[2] * pltpu.roll(x, 1, 1) + a[3] * pltpu.roll(x, 7, 0))
                + a[4] * pltpu.roll(x, 1, 0)
            )
            return carry

        loop(depth, body, 0)

    def completed(r, t, k, merged):
        rims = jnp.where(
            bottom_row, spread(s_in, r, t * padded + k), spread(n_in, r, t * padded + k)
        )
        return acc[at(t * depth + k), :] + (
            coef[5, at(k), :] * unpack(merged, k) + coef[6, at(k), :] * rims
        )

    def merged_of(r, t):
        return merge(lon_w[r, 8 * t:8 * t + 8, :], lon_e[r, 8 * t:8 * t + 8, :])

    def bands():
        loads[7].wait()
        upp[at(0), :] = zero
        low[at(0), :] = zero
        upp[at(depth), :] = zero
        low[at(depth), :] = zero

        def deeper(i, total):
            k = depth - 1 - i
            total = total + dv[at(k), :]
            flow = -float(PASSES) * total
            mixing = jnp.where(k.astype(F32) < count, fields[5, at(k - 1), :], 0.0)
            upp[at(k), :] = jnp.maximum(flow, 0.0) + mixing
            low[at(k), :] = mixing - jnp.minimum(flow, 0.0)
            return total

        loop(depth - 1, deeper, zero)

    def pivots(begin, size, q):
        def body(i, q):
            k = begin + i
            l, u = low[at(k), :], upp[at(k + 1), :]
            inv = 1.0 / (1.0 + low[at(k + 1), :] + upp[at(k), :] - l * q)
            q = u * inv
            ip[at(k), :] = inv
            mm[at(k), :] = l * inv
            qq[at(k), :] = q
            return q

        return loop(size, body, q)

    half = depth // 2
    interior(0)
    interior(1)
    for r in range(PASSES - 1):
        for t in range(2):
            wait_recv(r, t)
            merged = merged_of(r, t)

            def complete(k, packed):
                x = completed(r, t, k, merged)
                c[at(t * padded + k), :] = x
                return pack(x, k, packed)

            lon_out[r + 1, 8 * t:8 * t + 8, :] = loop(depth, complete, zero)
            stage_rows(r + 1, c, t * 8 * padded, t * padded)
            send(r + 1, t)
        interior(0)
        interior(1)
        if r == 0:
            bands()
        elif r == 1:
            q = pivots(0, half, zero)
        else:
            pivots(half, depth - half, q)

    merged = []
    for t in range(2):
        wait_recv(PASSES - 1, t)
        merged.append(merged_of(PASSES - 1, t))

    def forward(k, values):
        new = []
        for t in range(2):
            x = completed(PASSES - 1, t, k, merged[t])
            v = x * ip[at(k), :] + mm[at(k), :] * values[t]
            res[at(t * depth + k), :] = v
            new.append(v)
        return tuple(new)

    values = loop(depth, forward, (zero, zero))

    def backward(i, values):
        k = depth - 1 - i
        q = qq[at(k), :]
        new = []
        for t, out in enumerate((out_t, out_s)):
            x = res[at(t * depth + k), :] + q * values[t]
            out[at(k), :] = x
            new.append(x)
        return tuple(new)

    loop(depth, backward, (zero, zero))
    for r in range(PASSES):
        for g in range(3 if r == 0 else 2):
            wait_send(r, g)


def solution(mesh):
    nlon, nlat = mesh.shape["lon"], mesh.shape["lat"]
    cube, plane = P(None, "lat", "lon"), P("lat", "lon")

    def shards(*args):
        depth = args[0].shape[0]
        padded = -(-depth // 8) * 8
        rows = 8 * depth
        flat = [a.reshape(rows, 128) for a in args[:6]] + list(args[6:])
        edge_rows = 8 + 3 * padded
        vmem = pltpu.VMEM
        scratch = [
            vmem((6, rows, 128), F32), vmem((2, 8, 128), jnp.int32),
            vmem((16 * padded, 128), F32), vmem((2 * rows, 128), F32),
            vmem((rows, 128), F32), vmem((8 * padded, 128), F32),
            vmem((7, rows, 128), F32), vmem((rows, 128), F32),
            vmem((rows + 8, 128), F32), vmem((rows + 8, 128), F32),
            vmem((rows, 128), F32), vmem((rows, 128), F32), vmem((rows, 128), F32),
            vmem((2 * rows, 128), F32),
        ]
        scratch += [vmem((PASSES, 24, 128), F32) for _ in range(3)]
        scratch += [vmem((PASSES, edge_rows, 128), F32) for _ in range(4)]
        scratch += [
            pltpu.SemaphoreType.DMA((8,)), pltpu.SemaphoreType.DMA((PASSES, 3, 4)),
            pltpu.SemaphoreType.DMA((PASSES, 3, 4)),
        ]
        outs = pl.pallas_call(
            functools.partial(tracer_kernel, nlon, nlat, depth),
            out_shape=[jax.ShapeDtypeStruct((rows, 128), F32)] * 2,
            in_specs=[pl.BlockSpec(memory_space=pltpu.HBM)] * 8,
            out_specs=[pl.BlockSpec(memory_space=pltpu.VMEM)] * 2,
            scratch_shapes=scratch,
            compiler_params=pltpu.CompilerParams(
                collective_id=0, has_side_effects=True, vmem_limit_bytes=56 * 1024 * 1024
            ),
            cost_estimate=pl.CostEstimate(flops=20000000, bytes_accessed=1600000, transcendentals=0),
            name="tracer_step",
        )(*flat)
        return tuple(o.reshape(depth, 8, 128) for o in outs)

    return jax.shard_map(
        shards, mesh=mesh, in_specs=(cube,) * 6 + (plane,) * 2, out_specs=(cube, cube), check_vma=False
    )
```

time: 30.4 us -> 23.6 us (0.78)
  local copies, waits for them, and re-layouts: 7.58 us -> 2.33 us
  Pallas kernels: 21.8 us -> 20.5 us
    unnamed x18 -> x4, local copies, waits for them, and re-layouts: 7.58 us -> 2.33 us
    pallas_call x1, Pallas kernels: 21.8 us -> 20.5 us  [shards(): pl.pallas_call(functools.partial(tracer_kernel, nlon, nlat, depth), out_s...]
where the time goes in v2:
time: 23.6 us; the launch traced here: 23.4 us
  Pallas kernels  20.5 us (87%)
  local copies, waits for them, and re-layouts  2.33 us (10%)
  between operations  0.65 us (3%)
    pallas_call x1, Pallas kernels, shards(): pl.pallas_call(functools.partial(tracer_kernel, nlon, nlat, depth), out_s...  20.5 us
    unnamed x4, local copies, waits for them, and re-layouts  2.33 us

profile of v2, /device:TPU:0, one launch (start us, length us, event | category | flops | bytes accessed | tf_op | source)
XLA Modules:
  0.0 23.4 jit_solution(6779799299310312067)
XLA Ops:
  0.6 20.5 %tracer_step.1 = (f32[368,128]{1,0:T(8,128)}, f32[368,128]{1,0:T(8,128)}) custom-call(f32[368,128]{1,0:T(8,128)} %bitcast.8, f32[368,128]{1,0:T(8,128)} %bitcast.9, f32[368,128]{1,0:T(8,128)} %bitcast.10, f32[368,128]{1,0:T(8,128)} %bitcast.11, f32[368,128]{1,0:T(8,128)} %bitcast.12, f32[368,128]{1,0:T(8,128)} %bitcast.13, s32[8,128]{1,0:T(8,128)} %ind.1, ...), custom_call_target="tpu_custom_call" | custom-call | flops 20000000 | bytes 1600000 | tf_op jit(solution)/shard_map/tracer_step/pallas_call | solution.py:382
  21.1 0.0 copy-start
  21.1 1.6 %copy.12 = f32[46,8,128]{2,1,0:T(8,128)} copy(f32[46,8,128]{2,1,0:T(8,128)} %bitcast.15) | data formatting | bytes 376832
  22.8 0.0 copy-done
  22.8 0.7 %copy.13 = f32[46,8,128]{2,1,0:T(8,128)} copy(f32[46,8,128]{2,1,0:T(8,128)S(1)} %bitcast.14) | data formatting | bytes 376832
Async XLA Ops:
  21.1 1.7 %copy-start = (f32[368,128]{1,0:T(8,128)S(1)}, f32[368,128]{1,0:T(8,128)}, u32[]{:S(2)}) copy-start(f32[368,128]{1,0:T(8,128)} %get-tuple-element.5) | copy-start | bytes 565252

commit v3 on v2

--- a/solution.py
+++ b/solution.py
@@ -25,6 +25,7 @@
     lon = lax.axis_index("lon")
     lat = lax.axis_index("lat")
     is_top = lat == nlat - 1
+    part = -(-depth // 2)
     east = lax.rem(lon + 1, nlon)
     west = lax.rem(lon + nlon - 1, nlon)
     mirror = nlon - 1 - lon
@@ -71,8 +72,8 @@
     def at(k):
         return pl.ds(pl.multiple_of(k * 8, 8), 8)
 
-    def loop(count, body, init):
-        return lax.fori_loop(0, count, body, init, unroll=count)
+    def loop(count, body, init, unroll=None):
+        return lax.fori_loop(0, count, body, init, unroll=count if unroll is None else unroll)
 
     def pack(x, k, packed):
         return jnp.where(pair == k, pltpu.roll(x, 2 * k + 1, 1), packed)
@@ -190,7 +191,7 @@
         nf[at(k), :] = fields[2, at(k), :] * drag
         return pack(e, k, packed)
 
-    lon_out[0, 16:24, :] = pack(count, depth, loop(depth, flows, zero))
+    lon_out[0, 16:24, :] = pack(count, depth, loop(depth, flows, zero, part))
     n_out[0, pl.ds(2 * padded, 8), :] = turn(jnp.broadcast_to(count[7:8, :], (8, 128)))
     s_out[0, pl.ds(2 * padded, 8), :] = jnp.broadcast_to(count[0:1, :], (8, 128))
     stage_rows(0, nf, 0, 2 * padded + 8)
@@ -239,7 +240,7 @@
         dv[at(k), :] = fe - fw + fn - fs
         return carry
 
-    loop(depth, faces, 0)
+    loop(depth, faces, 0, part)
 
     def interior(t):
         def body(k, carry):
@@ -281,9 +282,11 @@
             low[at(k), :] = mixing - jnp.minimum(flow, 0.0)
             return total
 
-        loop(depth - 1, deeper, zero)
-
-    def pivots(begin, size, q):
+        loop(depth - 1, deeper, zero, 5)
+
+    def pivots(begin, size):
+        q = qq[at(jnp.int32(begin - 1)), :] if begin else zero
+
         def body(i, q):
             k = begin + i
             l, u = low[at(k), :], upp[at(k + 1), :]
@@ -294,13 +297,19 @@
             qq[at(k), :] = q
             return q
 
-        return loop(size, body, q)
+        loop(size, body, q, 4)
 
     half = depth // 2
-    interior(0)
-    interior(1)
-    for r in range(PASSES - 1):
+    wait_send(0, 2)
+
+    def substep(r, carry):
+        interior(0)
+        interior(1)
+        pl.when(r == 0)(bands)
+        pl.when(r == 1)(lambda: pivots(0, half))
+        pl.when(r == 2)(lambda: pivots(half, depth - half))
         for t in range(2):
+            wait_send(r, t)
             wait_recv(r, t)
             merged = merged_of(r, t)
 
@@ -312,14 +321,11 @@
             lon_out[r + 1, 8 * t:8 * t + 8, :] = loop(depth, complete, zero)
             stage_rows(r + 1, c, t * 8 * padded, t * padded)
             send(r + 1, t)
-        interior(0)
-        interior(1)
-        if r == 0:
-            bands()
-        elif r == 1:
-            q = pivots(0, half, zero)
-        else:
-            pivots(half, depth - half, q)
+        return carry
+
+    lax.fori_loop(0, PASSES - 1, substep, 0)
+    interior(0)
+    interior(1)
 
     merged = []
     for t in range(2):
@@ -348,9 +354,8 @@
         return tuple(new)
 
     loop(depth, backward, (zero, zero))
-    for r in range(PASSES):
-        for g in range(3 if r == 0 else 2):
-            wait_send(r, g)
+    for t in range(2):
+        wait_send(PASSES - 1, t)
 
 
 def solution(mesh):
@@ -386,7 +391,7 @@
             out_specs=[pl.BlockSpec(memory_space=pltpu.VMEM)] * 2,
             scratch_shapes=scratch,
             compiler_params=pltpu.CompilerParams(
-                collective_id=0, has_side_effects=True, vmem_limit_bytes=56 * 1024 * 1024
+                collective_id=0, has_side_effects=True, vmem_limit_bytes=54784 * 1024
             ),
             cost_estimate=pl.CostEstimate(flops=20000000, bytes_accessed=1600000, transcendentals=0),
             name="tracer_step",

time: 23.6 us -> 23.1 us (0.979)
  Pallas kernels: 20.5 us -> 20.2 us
  local copies, waits for them, and re-layouts: 2.33 us -> 2.04 us
    pallas_call x1, Pallas kernels: 20.5 us -> 20.2 us  [shards(): pl.pallas_call(functools.partial(tracer_kernel, nlon, nlat, depth), out_s...]
    unnamed x4 -> x6, local copies, waits for them, and re-layouts: 2.33 us -> 2.04 us
where the time goes in v3:
time: 23.1 us; the launch traced here: 22.9 us
  Pallas kernels  20.2 us (87%)
  local copies, waits for them, and re-layouts  2.04 us (9%)
  between operations  0.66 us (3%)
    pallas_call x1, Pallas kernels, shards(): pl.pallas_call(functools.partial(tracer_kernel, nlon, nlat, depth), out_s...  20.2 us
    unnamed x6, local copies, waits for them, and re-layouts  2.04 us

profile of v3, /device:TPU:0, one launch (start us, length us, event | category | flops | bytes accessed | tf_op | source)
XLA Modules:
  0.0 22.9 jit_solution(9992383641503387845)
XLA Ops:
  0.6 0.0 copy-start.1
  0.6 0.0 copy-start
  0.7 0.7 %copy-done.1 = s32[8,128]{1,0:T(8,128)S(1)} copy-done((s32[8,128]{1,0:T(8,128)S(1)}, s32[8,128]{1,0:T(8,128)}, u32[]{:S(2)}) %copy-start.1) | copy-done | bytes 4120
  1.3 0.0 copy-done
  1.3 20.2 %tracer_step.1 = (f32[368,128]{1,0:T(8,128)S(1)}, f32[368,128]{1,0:T(8,128)S(1)}) custom-call(f32[368,128]{1,0:T(8,128)} %bitcast.10, f32[368,128]{1,0:T(8,128)} %bitcast.11, f32[368,128]{1,0:T(8,128)} %bitcast.12, f32[368,128]{1,0:T(8,128)} %bitcast.13, f32[368,128]{1,0:T(8,128)} %bitcast.14, f32[368,128]{1,0:T(8,128)} %bitcast.15, s32[8,128]{1,0:T(8,128)S(1)} %copy-done, ...), custom_call_target="tpu_custom_call" | custom-call | flops 20000000 | bytes 1600000 | tf_op jit(solution)/shard_map/tracer_step/pallas_call | solution.py:387
  21.5 0.7 %copy.12 = f32[46,8,128]{2,1,0:T(8,128)} copy(f32[46,8,128]{2,1,0:T(8,128)S(1)} %bitcast.9) | data formatting | bytes 376832
  22.2 0.7 %copy.13 = f32[46,8,128]{2,1,0:T(8,128)} copy(f32[46,8,128]{2,1,0:T(8,128)S(1)} %bitcast.8) | data formatting | bytes 376832
Async XLA Ops:
  0.6 0.7 %copy-start.1 = (s32[8,128]{1,0:T(8,128)S(1)}, s32[8,128]{1,0:T(8,128)}, u32[]{:S(2)}) copy-start(s32[8,128]{1,0:T(8,128)} %dep.1) | copy-start | bytes 12292
  0.6 0.7 %copy-start = (s32[8,128]{1,0:T(8,128)S(1)}, s32[8,128]{1,0:T(8,128)}, u32[]{:S(2)}) copy-start(s32[8,128]{1,0:T(8,128)} %ind.1) | copy-start | bytes 12292

commit v4 on v3

--- a/solution.py
+++ b/solution.py
@@ -217,6 +217,14 @@
     least_s = jnp.minimum(count, jnp.where(bottom_row, s_in[0, pl.ds(2 * padded, 8), :], pltpu.roll(count, 1, 0)))
     least_n = jnp.minimum(count, jnp.where(top_row, n_in[0, pl.ds(2 * padded, 8), :], pltpu.roll(count, 7, 0)))
 
+    def inside(a, t, k):
+        x = c[at(t * padded + k), :]
+        acc[at(t * depth + k), :] = (
+            (a[0] * x + a[1] * pltpu.roll(x, 127, 1))
+            + (a[2] * pltpu.roll(x, 1, 1) + a[3] * pltpu.roll(x, 7, 0))
+            + a[4] * pltpu.roll(x, 1, 0)
+        )
+
     def faces(k, carry):
         level = k.astype(F32)
         e, n = ef[at(k), :], nf[at(k), :]
@@ -230,11 +238,17 @@
         dn, ds = jnp.where(on, DIFFUSE, 0.0), jnp.where(os, DIFFUSE, 0.0)
         ne, pw = de - jnp.minimum(fe, 0.0), jnp.maximum(fw, 0.0) + dw
         nn, p_s = dn - jnp.minimum(fn, 0.0), jnp.maximum(fs, 0.0) + ds
-        coef[0, at(k), :] = 1.0 - ((fe + ne) + (pw - fw) + (fn + nn) + (p_s - fs))
-        coef[1, at(k), :] = jnp.where(last, 0.0, ne)
-        coef[2, at(k), :] = jnp.where(first, 0.0, pw)
-        coef[3, at(k), :] = jnp.where(top_row, 0.0, nn)
-        coef[4, at(k), :] = jnp.where(bottom_row, 0.0, p_s)
+        a = (
+            1.0 - ((fe + ne) + (pw - fw) + (fn + nn) + (p_s - fs)),
+            jnp.where(last, 0.0, ne),
+            jnp.where(first, 0.0, pw),
+            jnp.where(top_row, 0.0, nn),
+            jnp.where(bottom_row, 0.0, p_s),
+        )
+        for i, values in enumerate(a):
+            coef[i, at(k), :] = values
+        for t in range(2):
+            inside(a, t, k)
         coef[5, at(k), :] = jnp.where(first, pw, jnp.where(last, ne, 0.0))
         coef[6, at(k), :] = jnp.where(bottom_row, p_s, jnp.where(top_row, nn, 0.0))
         dv[at(k), :] = fe - fw + fn - fs
@@ -244,13 +258,7 @@
 
     def interior(t):
         def body(k, carry):
-            a = [coef[i, at(k), :] for i in range(5)]
-            x = c[at(t * padded + k), :]
-            acc[at(t * depth + k), :] = (
-                (a[0] * x + a[1] * pltpu.roll(x, 127, 1))
-                + (a[2] * pltpu.roll(x, 1, 1) + a[3] * pltpu.roll(x, 7, 0))
-                + a[4] * pltpu.roll(x, 1, 0)
-            )
+            inside([coef[i, at(k), :] for i in range(5)], t, k)
             return carry
 
         loop(depth, body, 0)
@@ -303,29 +311,27 @@
     wait_send(0, 2)
 
     def substep(r, carry):
+        for t in range(2):
+            wait_send(r, t)
+            wait_recv(r, t)
+            merged = merged_of(r, t)
+
+            def complete(k, packed):
+                x = completed(r, t, k, merged)
+                c[at(t * padded + k), :] = x
+                return pack(x, k, packed)
+
+            lon_out[r + 1, 8 * t:8 * t + 8, :] = loop(depth, complete, zero)
+            stage_rows(r + 1, c, t * 8 * padded, t * padded)
+            send(r + 1, t)
         interior(0)
         interior(1)
         pl.when(r == 0)(bands)
         pl.when(r == 1)(lambda: pivots(0, half))
         pl.when(r == 2)(lambda: pivots(half, depth - half))
-        for t in range(2):
-            wait_send(r, t)
-            wait_recv(r, t)
-            merged = merged_of(r, t)
-
-            def complete(k, packed):
-                x = completed(r, t, k, merged)
-                c[at(t * padded + k), :] = x
-                return pack(x, k, packed)
-
-            lon_out[r + 1, 8 * t:8 * t + 8, :] = loop(depth, complete, zero)
-            stage_rows(r + 1, c, t * 8 * padded, t * padded)
-            send(r + 1, t)
         return carry
 
     lax.fori_loop(0, PASSES - 1, substep, 0)
-    interior(0)
-    interior(1)
 
     merged = []
     for t in range(2):

time: 23.1 us -> 22.8 us (0.987)
  Pallas kernels: 20.2 us -> 19.9 us
where the time goes in v4:
time: 22.8 us; the launch traced here: 22.6 us
  Pallas kernels  19.9 us (87%)
  local copies, waits for them, and re-layouts  2.04 us (9%)
  between operations  0.66 us (3%)
    pallas_call x1, Pallas kernels, shards(): pl.pallas_call(functools.partial(tracer_kernel, nlon, nlat, depth), out_s...  19.9 us
    unnamed x6, local copies, waits for them, and re-layouts  2.04 us

profile of v4, /device:TPU:0, one launch (start us, length us, event | category | flops | bytes accessed | tf_op | source)
XLA Modules:
  0.0 22.6 jit_solution(9424310928997890806)
XLA Ops:
  0.6 0.0 copy-start.1
  0.6 0.0 copy-start
  0.7 0.7 %copy-done.1 = s32[8,128]{1,0:T(8,128)S(1)} copy-done((s32[8,128]{1,0:T(8,128)S(1)}, s32[8,128]{1,0:T(8,128)}, u32[]{:S(2)}) %copy-start.1) | copy-done | bytes 4120
  1.3 0.0 copy-done
  1.3 19.9 %tracer_step.1 = (f32[368,128]{1,0:T(8,128)S(1)}, f32[368,128]{1,0:T(8,128)S(1)}) custom-call(f32[368,128]{1,0:T(8,128)} %bitcast.10, f32[368,128]{1,0:T(8,128)} %bitcast.11, f32[368,128]{1,0:T(8,128)} %bitcast.12, f32[368,128]{1,0:T(8,128)} %bitcast.13, f32[368,128]{1,0:T(8,128)} %bitcast.14, f32[368,128]{1,0:T(8,128)} %bitcast.15, s32[8,128]{1,0:T(8,128)S(1)} %copy-done, ...), custom_call_target="tpu_custom_call" | custom-call | flops 20000000 | bytes 1600000 | tf_op jit(solution)/shard_map/tracer_step/pallas_call | solution.py:393
  21.3 0.7 %copy.12 = f32[46,8,128]{2,1,0:T(8,128)} copy(f32[46,8,128]{2,1,0:T(8,128)S(1)} %bitcast.9) | data formatting | bytes 376832
  22.0 0.7 %copy.13 = f32[46,8,128]{2,1,0:T(8,128)} copy(f32[46,8,128]{2,1,0:T(8,128)S(1)} %bitcast.8) | data formatting | bytes 376832
Async XLA Ops:
  0.6 0.7 %copy-start.1 = (s32[8,128]{1,0:T(8,128)S(1)}, s32[8,128]{1,0:T(8,128)}, u32[]{:S(2)}) copy-start(s32[8,128]{1,0:T(8,128)} %dep.1) | copy-start | bytes 12292
  0.6 0.7 %copy-start = (s32[8,128]{1,0:T(8,128)S(1)}, s32[8,128]{1,0:T(8,128)}, u32[]{:S(2)}) copy-start(s32[8,128]{1,0:T(8,128)} %ind.1) | copy-start | bytes 12292

commit v5 on v4

--- a/solution.py
+++ b/solution.py
@@ -138,6 +138,7 @@
         def _():
             to_south(r, g).start()
 
+    def send_sides(r, g):
         to_east(r, g).start()
         to_west(r, g).start()
 
@@ -196,6 +197,7 @@
     s_out[0, pl.ds(2 * padded, 8), :] = jnp.broadcast_to(count[0:1, :], (8, 128))
     stage_rows(0, nf, 0, 2 * padded + 8)
     pl.semaphore_wait(barrier, 3 + jnp.where(lat > 0, 1, 0))
+    send_sides(0, 2)
     send(0, 2)
     for t in range(2):
         loads[5 + t].wait()
@@ -206,6 +208,7 @@
             return pack(x, k, packed)
 
         lon_out[0, 8 * t:8 * t + 8, :] = loop(depth, masked, zero)
+        send_sides(0, t)
         stage_rows(0, c, t * 8 * padded, t * padded)
         send(0, t)
     wait_recv(0, 2)
@@ -322,6 +325,7 @@
                 return pack(x, k, packed)
 
             lon_out[r + 1, 8 * t:8 * t + 8, :] = loop(depth, complete, zero)
+            send_sides(r + 1, t)
             stage_rows(r + 1, c, t * 8 * padded, t * padded)
             send(r + 1, t)
         interior(0)

time: 22.8 us -> 23.1 us (1.013)
  Pallas kernels: 19.9 us -> 20.2 us
where the time goes in v5:
time: 23.1 us; the launch traced here: 22.8 us
  Pallas kernels  20.2 us (87%)
  local copies, waits for them, and re-layouts  2.04 us (9%)
  between operations  0.66 us (3%)
    pallas_call x1, Pallas kernels, shards(): pl.pallas_call(functools.partial(tracer_kernel, nlon, nlat, depth), out_s...  20.2 us
    unnamed x6, local copies, waits for them, and re-layouts  2.04 us

profile of v5, /device:TPU:0, one launch (start us, length us, event | category | flops | bytes accessed | tf_op | source)
XLA Modules:
  0.0 22.8 jit_solution(3883932213968588428)
XLA Ops:
  0.6 0.0 copy-start.1
  0.6 0.0 copy-start
  0.7 0.7 %copy-done.1 = s32[8,128]{1,0:T(8,128)S(1)} copy-done((s32[8,128]{1,0:T(8,128)S(1)}, s32[8,128]{1,0:T(8,128)}, u32[]{:S(2)}) %copy-start.1) | copy-done | bytes 4120
  1.3 0.0 copy-done
  1.3 20.2 %tracer_step.1 = (f32[368,128]{1,0:T(8,128)S(1)}, f32[368,128]{1,0:T(8,128)S(1)}) custom-call(f32[368,128]{1,0:T(8,128)} %bitcast.10, f32[368,128]{1,0:T(8,128)} %bitcast.11, f32[368,128]{1,0:T(8,128)} %bitcast.12, f32[368,128]{1,0:T(8,128)} %bitcast.13, f32[368,128]{1,0:T(8,128)} %bitcast.14, f32[368,128]{1,0:T(8,128)} %bitcast.15, s32[8,128]{1,0:T(8,128)S(1)} %copy-done, ...), custom_call_target="tpu_custom_call" | custom-call | flops 20000000 | bytes 1600000 | tf_op jit(solution)/shard_map/tracer_step/pallas_call | solution.py:397
  21.5 0.7 %copy.12 = f32[46,8,128]{2,1,0:T(8,128)} copy(f32[46,8,128]{2,1,0:T(8,128)S(1)} %bitcast.9) | data formatting | bytes 376832
  22.2 0.7 %copy.13 = f32[46,8,128]{2,1,0:T(8,128)} copy(f32[46,8,128]{2,1,0:T(8,128)S(1)} %bitcast.8) | data formatting | bytes 376832
Async XLA Ops:
  0.6 0.7 %copy-start.1 = (s32[8,128]{1,0:T(8,128)S(1)}, s32[8,128]{1,0:T(8,128)}, u32[]{:S(2)}) copy-start(s32[8,128]{1,0:T(8,128)} %dep.1) | copy-start | bytes 12292
  0.6 0.7 %copy-start = (s32[8,128]{1,0:T(8,128)S(1)}, s32[8,128]{1,0:T(8,128)}, u32[]{:S(2)}) copy-start(s32[8,128]{1,0:T(8,128)} %ind.1) | copy-start | bytes 12292

commit v6 on v4

--- a/solution.py
+++ b/solution.py
@@ -333,21 +333,17 @@
 
     lax.fori_loop(0, PASSES - 1, substep, 0)
 
-    merged = []
     for t in range(2):
         wait_recv(PASSES - 1, t)
-        merged.append(merged_of(PASSES - 1, t))
-
-    def forward(k, values):
-        new = []
-        for t in range(2):
-            x = completed(PASSES - 1, t, k, merged[t])
-            v = x * ip[at(k), :] + mm[at(k), :] * values[t]
+        merged = merged_of(PASSES - 1, t)
+
+        def forward(k, value):
+            x = completed(PASSES - 1, t, k, merged)
+            v = x * ip[at(k), :] + mm[at(k), :] * value
             res[at(t * depth + k), :] = v
-            new.append(v)
-        return tuple(new)
-
-    values = loop(depth, forward, (zero, zero))
+            return v
+
+        loop(depth, forward, zero)
 
     def backward(i, values):
         k = depth - 1 - i

time: 22.8 us -> 22.8 us (level)
  no operation moved by 1% of the time
where the time goes in v6:
time: 22.8 us; the launch traced here: 22.6 us
  Pallas kernels  19.9 us (87%)
  local copies, waits for them, and re-layouts  2.04 us (9%)
  between operations  0.66 us (3%)
    pallas_call x1, Pallas kernels, shards(): pl.pallas_call(functools.partial(tracer_kernel, nlon, nlat, depth), out_s...  19.9 us
    unnamed x6, local copies, waits for them, and re-layouts  2.04 us

profile of v6, /device:TPU:0, one launch (start us, length us, event | category | flops | bytes accessed | tf_op | source)
XLA Modules:
  0.0 22.6 jit_solution(744526132549612905)
XLA Ops:
  0.6 0.0 copy-start.1
  0.6 0.0 copy-start
  0.7 0.7 %copy-done.1 = s32[8,128]{1,0:T(8,128)S(1)} copy-done((s32[8,128]{1,0:T(8,128)S(1)}, s32[8,128]{1,0:T(8,128)}, u32[]{:S(2)}) %copy-start.1) | copy-done | bytes 4120
  1.3 0.0 copy-done
  1.3 19.9 %tracer_step.1 = (f32[368,128]{1,0:T(8,128)S(1)}, f32[368,128]{1,0:T(8,128)S(1)}) custom-call(f32[368,128]{1,0:T(8,128)} %bitcast.10, f32[368,128]{1,0:T(8,128)} %bitcast.11, f32[368,128]{1,0:T(8,128)} %bitcast.12, f32[368,128]{1,0:T(8,128)} %bitcast.13, f32[368,128]{1,0:T(8,128)} %bitcast.14, f32[368,128]{1,0:T(8,128)} %bitcast.15, s32[8,128]{1,0:T(8,128)S(1)} %copy-done, ...), custom_call_target="tpu_custom_call" | custom-call | flops 20000000 | bytes 1600000 | tf_op jit(solution)/shard_map/tracer_step/pallas_call | solution.py:389
  21.3 0.7 %copy.12 = f32[46,8,128]{2,1,0:T(8,128)} copy(f32[46,8,128]{2,1,0:T(8,128)S(1)} %bitcast.9) | data formatting | bytes 376832
  22.0 0.7 %copy.13 = f32[46,8,128]{2,1,0:T(8,128)} copy(f32[46,8,128]{2,1,0:T(8,128)S(1)} %bitcast.8) | data formatting | bytes 376832
Async XLA Ops:
  0.6 0.7 %copy-start.1 = (s32[8,128]{1,0:T(8,128)S(1)}, s32[8,128]{1,0:T(8,128)}, u32[]{:S(2)}) copy-start(s32[8,128]{1,0:T(8,128)} %dep.1) | copy-start | bytes 12292
  0.6 0.7 %copy-start = (s32[8,128]{1,0:T(8,128)S(1)}, s32[8,128]{1,0:T(8,128)}, u32[]{:S(2)}) copy-start(s32[8,128]{1,0:T(8,128)} %ind.1) | copy-start | bytes 12292
